TPU v7x, 128 devices: a whole 4x4x4 slice. The times are simulated.
128 devices in a mesh: dp: 8 (over z_hi, x), tensor: 16 (over y, z_lo, core).
Axes of the slice: x: 4, y: 4, z: 4 (z_hi: 2, z_lo: 2; z = z_hi * 2 + z_lo), core: 2. Of those that a mesh axis runs over, the one named last changes fastest.
Arguments:
- tokens: bfloat16 [2048, 4608], P(('dp', 'tensor')), may hold values from -6 to 6
- tangent: bfloat16 [2048, 4608], P(('dp', 'tensor')), may hold values from -6 to 6
- hessian_weight: float32 [2048], P('dp'), may hold values from 0.02 to 0.2
- gate_weight: bfloat16 [4608, 18432], P(None, 'tensor'), may hold values from -0.09375 to 0.09375
- up_weight: bfloat16 [4608, 18432], P(None, 'tensor'), may hold values from -0.09375 to 0.09375
- down_weight: bfloat16 [18432, 4608], P('tensor', 'dp'), may hold values from -0.046875 to 0.046875
Outputs:
- layer_out: bfloat16 [2048, 4608], P(('dp', 'tensor'))
- out_tangent: bfloat16 [2048, 4608], P(('dp', 'tensor'))
- curvature: bfloat16 [18432, 4608], P('tensor', 'dp')
All inputs are finite; a program needn't handle non-finite values.
Results may differ from a plain program's by a relative error of at most 0.03.
Values may be sent and summed in bfloat16 or wider, within the bound.
No kernel may reach another device: no remote copies, remote signals or barrier semaphores. Data moves between devices by JAX's collectives and lax.ppermute only.
A program may use at most 192 MiB of HBM per device.

v0:
```python
import jax
import jax.numpy as jnp
from jax import lax
from jax.experimental import pallas as pl
from jax.experimental.pallas import tpu as pltpu
from jax.sharding import PartitionSpec as P

gelu_scale = 0.7978845608
cubic_coeff = 0.044715


def fetch_t(value, ky=0, kz=0, kc=0):
    key = ky * 4 + kz * 2 + kc
    return lax.ppermute(value, "tensor", [(i ^ key, i) for i in range(16)])


def fetch_d(value, kh=0, kx=0):
    key = kh * 4 + kx
    return lax.ppermute(value, "dp", [(i ^ key, i) for i in range(8)])


def after(value, *done):
    def nothing(*refs):
        del refs

    anywhere = pl.BlockSpec(memory_space=pl.ANY)
    return pl.pallas_call(
        nothing,
        out_shape=jax.ShapeDtypeStruct(value.shape, value.dtype),
        in_specs=[anywhere] * (1 + len(done)),
        out_specs=anywhere,
        input_output_aliases={0: 0},
        compiler_params=pltpu.CompilerParams(vmem_limit_bytes=1 << 17),
    )(value, *done)


def exchange_x(value):
    return fetch_d(value, kx=1), fetch_d(value, kx=3)


def far_x(one, three):
    half = one.shape[0] // 2
    return fetch_d(three[:half], kx=1), fetch_d(one[half:], kx=3)


def gather_y(pair):
    one = fetch_t(pair, ky=1)
    three = fetch_t(pair, ky=3)
    return one, three, (fetch_t(three[:1], ky=1), fetch_t(one[1:], ky=3))


def core_sum(partial):
    other = fetch_t(partial[:, 1], kc=1)
    return partial[:, 0].astype(jnp.float32) + other.astype(jnp.float32)


def column_sum(chip, ready=()):
    column = after(chip[:, 0], *ready) if ready else chip[:, 0]
    for key, place in ((2, 3), (1, 1), (3, 2)):
        got = fetch_t(chip[:, place].astype(jnp.bfloat16), ky=key)
        column = column + got.astype(jnp.float32)
    return column


def side_sum(column):
    first = fetch_t(column[:, 0, ::-1].astype(jnp.bfloat16), kz=1)
    second = fetch_t(column[:, 1, 1].astype(jnp.bfloat16), kz=1)
    return (
        column[:, 0] + first.astype(jnp.float32),
        column[:, 1, 0] + second.astype(jnp.float32),
    )


def gelu_pair(values_in):
    inner_arg = gelu_scale * (values_in + cubic_coeff * values_in * values_in * values_in)
    tanh_term = jnp.tanh(inner_arg)
    activated = 0.5 * values_in * (1.0 + tanh_term)
    gelu_slope = 0.5 * (1.0 + tanh_term) + 0.5 * values_in * (
        1.0 - tanh_term * tanh_term
    ) * gelu_scale * (1.0 + 3.0 * cubic_coeff * values_in * values_in)
    return (activated, gelu_slope)


def gate_of(own, other, gate_weight):
    flat = jnp.concatenate((*own, *other))
    flat = flat.reshape(-1, flat.shape[-1])
    return flat, jnp.dot(flat, gate_weight, preferred_element_type=jnp.float32)


def hidden_of(flat, gate, up_weight, rows):
    up = jnp.dot(flat, up_weight, preferred_element_type=jnp.float32)
    gate = gate.reshape(-1, 2, rows, gate.shape[1])
    up = up.reshape(-1, 2, rows, up.shape[1])
    activated, gelu_slope = gelu_pair(gate[:, 0])
    hidden = activated * up[:, 0]
    tangent = gelu_slope * gate[:, 1] * up[:, 0] + activated * up[:, 1]
    both = jnp.stack((tangent.astype(jnp.bfloat16), hidden.astype(jnp.bfloat16)))
    return both.reshape(2, 2, -1, gate.shape[-1])


def product(left, blocks, rows):
    groups = left.shape[0]
    left = left.reshape(-1, left.shape[-1])
    height, depth = left.shape
    columns = sum(block.shape[0] for block in blocks)
    tile = 256 if columns % 256 == 0 else columns
    n_block = len(blocks)

    def kernel(left_ref, *refs):
        out_ref, right_ref, sems = refs[-3:]
        copies, place = [], 0
        for k, block in enumerate(refs[:n_block]):
            size = block.shape[0]
            copy = pltpu.make_async_copy(block, right_ref.at[pl.ds(place, size)], sems.at[k])
            copy.start()
            copies.append((place, copy))
            place += size
        for at in range(0, columns, tile):
            while copies and copies[0][0] < at + tile:
                copies.pop(0)[1].wait()
            total = lax.dot_general(
                left_ref[...],
                right_ref[at : at + tile, :],
                (((1,), (1,)), ((), ())),
                preferred_element_type=jnp.float32,
            )
            out_ref[:, at : at + tile] = total.astype(jnp.bfloat16)

    near = pl.BlockSpec(memory_space=pltpu.VMEM)
    anywhere = pl.BlockSpec(memory_space=pl.ANY)
    out = pl.pallas_call(
        kernel,
        out_shape=jax.ShapeDtypeStruct((height, columns), jnp.bfloat16),
        in_specs=[near] + [anywhere] * n_block,
        out_specs=near,
        scratch_shapes=[
            pltpu.VMEM((columns, depth), jnp.bfloat16),
            pltpu.SemaphoreType.DMA((n_block,)),
        ],
        compiler_params=pltpu.CompilerParams(vmem_limit_bytes=16 << 20),
        cost_estimate=pl.CostEstimate(
            flops=2 * height * depth * columns,
            bytes_accessed=2 * columns * (depth + height),
            transcendentals=0,
        ),
    )(left, *blocks)
    return out.reshape(groups, 2, 4, 2, rows, columns)


def outer_sum(parts, blocks):
    rows, columns = parts[0].shape[-2:]
    width = blocks[0].shape[-1]
    parts = [part.reshape(-1, columns) for part in parts]
    blocks = [block.reshape(-1, rows, width) for block in blocks]
    pieces, n_block = blocks[0].shape[0], len(blocks)
    tokens = pieces * n_block * rows
    size = parts[0].shape[0]
    tile = 384 if width % 384 == 0 else width

    def kernel(*refs):
        out_ref, weighted_ref, hidden_ref, sems = refs[-4:]
        copies = []
        for k, part in enumerate(refs[: len(parts)]):
            target = weighted_ref.at[pl.ds(k * size, size)]
            copies.append(pltpu.make_async_copy(part, target, sems.at[k]))
        for k, block in enumerate(refs[len(parts) : len(parts) + n_block]):
            target = hidden_ref.at[:, k]
            copies.append(pltpu.make_async_copy(block, target, sems.at[len(parts) + k]))
        for copy in copies:
            copy.start()
        for copy in copies:
            copy.wait()
        for at in range(0, width, tile):
            total = lax.dot_general(
                weighted_ref[...],
                hidden_ref[:, :, :, at : at + tile].reshape(tokens, tile),
                (((0,), (0,)), ((), ())),
                preferred_element_type=jnp.float32,
            )
            out_ref[:, at : at + tile] = total.astype(jnp.bfloat16)

    near = pl.BlockSpec(memory_space=pltpu.VMEM)
    anywhere = pl.BlockSpec(memory_space=pl.ANY)
    return pl.pallas_call(
        kernel,
        out_shape=jax.ShapeDtypeStruct((columns, width), jnp.bfloat16),
        in_specs=[anywhere] * (len(parts) + n_block),
        out_specs=near,
        scratch_shapes=[
            pltpu.VMEM((tokens, columns), jnp.bfloat16),
            pltpu.VMEM((pieces, n_block, rows, width), jnp.bfloat16),
            pltpu.SemaphoreType.DMA((len(parts) + n_block,)),
        ],
        compiler_params=pltpu.CompilerParams(vmem_limit_bytes=20 << 20),
        cost_estimate=pl.CostEstimate(
            flops=2 * tokens * columns * width,
            bytes_accessed=2 * (tokens * (columns + width) + columns * width),
            transcendentals=0,
        ),
    )(*parts, *blocks)


def whole_rows(own, other, place_h, place_x):
    block = own.shape[-1] // 4
    both = jnp.stack((own, other))
    b = [both[..., k * block : (k + 1) * block] for k in range(4)]
    odd = place_x & 1 == 1
    one = [jnp.where(odd, b[k ^ 1], b[k]) for k in range(4)]
    high = place_x & 2 == 2
    two = [jnp.where(high, one[k ^ 2], one[k]) for k in range(4)]
    second = place_h == 1
    halves = [[jnp.where(second, t[1 - h], t[h]) for t in two] for h in range(2)]
    return jnp.concatenate(halves[0] + halves[1], axis=-1)


def shards(tokens, tangent, hessian_weight, gate_weight, up_weight, down_weight):
    rows, width = tokens.shape
    place_d = lax.axis_index("dp")
    place_t = lax.axis_index("tensor")
    place_h, place_x = place_d // 4, place_d % 4

    piece = jnp.stack((tokens, tangent))
    pair = jnp.stack((piece, fetch_t(piece, kz=1)))
    pair_other = fetch_t(pair, kc=1)
    one, three, halves = gather_y(pair)
    one_other = fetch_t(one, kc=1)
    three_other = fetch_t(three, kc=1)

    down_0 = after(down_weight.T, piece)
    down_1, down_3 = exchange_x(down_0)
    down_lo, down_hi = far_x(down_1, down_3)
    down_half = (down_0, down_1, down_lo, down_hi, down_3)

    own_rows = jnp.stack(
        [
            lax.dynamic_slice_in_dim(hessian_weight, (place_t ^ key) * rows, rows, 0)
            for key in (0, 2)
        ]
    )

    flat, gate = gate_of((pair, one), (pair_other, one_other), gate_weight)
    two = jnp.concatenate([after(half, gate) for half in halves])
    two_other = fetch_t(two, kc=1)
    both_a = hidden_of(after(flat, gate, down_1, down_3), gate, up_weight, rows)
    both_a1 = fetch_d(both_a, kh=1)
    other_rows = fetch_d(after(own_rows, both_a), kh=1)
    two_other = after(two_other, both_a)
    both_b = hidden_of(
        *gate_of((three, two), (three_other, two_other), gate_weight), up_weight, rows
    )
    both_b1 = fetch_d(both_b, kh=1)
    both_0 = jnp.concatenate((both_a, both_b), axis=2)
    both_1 = jnp.concatenate((both_a1, both_b1), axis=2)

    hid_0, hid_1 = both_0[1], both_1[1]
    one_0, three_0 = exchange_x(hid_0)
    chip_0 = core_sum(product(after(both_0, both_a1, other_rows), down_half, rows))
    partial_1 = product(after(both_1, chip_0, one_0, three_0), down_half, rows)
    column_0 = column_sum(chip_0, (partial_1,))
    chip_1 = core_sum(partial_1)
    one_1, three_1 = exchange_x(after(hid_1, column_0))
    column_1 = column_sum(chip_1, (one_1, three_1))
    tan_rows, out_rows = side_sum(jnp.stack((column_0, column_1)))

    weight_rows = jnp.stack((own_rows, other_rows))
    weighted = (weight_rows[..., None] * tan_rows).astype(jnp.bfloat16)
    block = down_0.shape[0]
    parts = [weighted[..., :block]]
    for k in range(1, 4):
        parts.append(fetch_d(weighted[..., k * block : (k + 1) * block], kx=k))
    w_pair = jnp.stack(parts, axis=1)
    w_pair = w_pair.transpose(2, 0, 1, 3, 4)
    three_0, one_1 = after(three_0, w_pair), after(one_1, w_pair)
    two_0 = fetch_d(three_0, kx=1)
    two_1 = fetch_d(one_1, kx=3)
    hidden_all = (hid_0, one_0, two_0, three_0, both_1[1], one_1, two_1, three_1)

    w_one, w_three, halves = gather_y(w_pair)
    own = (w_pair, w_one, w_three, jnp.concatenate(halves))
    other = [fetch_t(part, kc=1) for part in own]
    swapped = other[0]
    blocks = [block.reshape(-1, rows, block.shape[-1]) for block in hidden_all]
    curvature = outer_sum((*own, *other), blocks).T

    sums = jnp.stack((tan_rows[:, 0], out_rows), axis=1).astype(jnp.bfloat16)
    others = fetch_d(after(sums[1], swapped), kh=1)
    out_tangent, layer_out = whole_rows(sums[0], others, place_h, place_x)
    return layer_out, out_tangent, curvature


def solution(mesh):
    placed = (
        P(("dp", "tensor"), None),
        P(("dp", "tensor"), None),
        P("dp"),
        P(None, "tensor"),
        P(None, "tensor"),
        P("tensor", "dp"),
    )
    return jax.shard_map(
        shards,
        mesh=mesh,
        in_specs=placed,
        out_specs=(P(("dp", "tensor"), None), P(("dp", "tensor"), None), P("tensor", "dp")),
        check_vma=False,
    )
```

profile of v0, /device:TPU:1, one launch (start us, length us, event | category | flops | bytes accessed | tf_op | source)
XLA Modules:
  0.0 177.1 jit_solution(16134077151611095151)
XLA Ops:
  0.7 1.4 copy.149
  2.1 2.5 %collective-permute-start = (bf16[2,16,4608]{2,1,0:T(8,128)(2,1)S(1)}, bf16[2,16,4608]{2,1,0:T(8,128)(2,1)}, u32[]{:S(2)}, u32[]{:S(2)}) collective-permute-start(bf16[2,16,4608]{2,1,0:T(8,128)(2,1)S(1)} %get-tuple-element.54.refs_1_), channel_id=1, source_target_pairs={{2,0},{3,1},{0,2},{1,3},{6,4},{7,5},{4,6},{5,7},{10,8},{11,9},{8,1... | collective-permute-start | bytes 884744 | tf_op jit(solution)/shard_map/ppermute | solution.py:14
  4.6 2.5 %collective-permute-start.5 = (bf16[576,1152]{1,0:T(8,128)(2,1)S(1)}, bf16[576,1152]{1,0:T(8,128)(2,1)S(1)}, u32[]{:S(2)}, u32[]{:S(2)}) collective-permute-start(bf16[576,1152]{1,0:T(8,128)(2,1)S(1)} %shard_map.85.refs_0_), channel_id=1, source_target_pairs={{48,0},{32,16},{16,32},{0,48},{112,64},{96,80},{80,96},{64,112},{4... | collective-permute-start | bytes 3981320 | tf_op jit(solution)/shard_map/ppermute | solution.py:19
  7.9 3.5 %collective-permute-done = bf16[2,16,4608]{2,1,0:T(8,128)(2,1)} collective-permute-done((bf16[2,16,4608]{2,1,0:T(8,128)(2,1)S(1)}, bf16[2,16,4608]{2,1,0:T(8,128)(2,1)}, u32[]{:S(2)}, u32[]{:S(2)}) %collective-permute-start) | collective-permute-done | bytes 294944 | tf_op jit(solution)/shard_map/ppermute | solution.py:14
  11.4 1.0 pad_maximum_fusion
  12.5 2.7 %collective-permute-start.6 = (bf16[2,2,16,4608]{3,2,1,0:T(8,128)(2,1)S(1)}, bf16[2,2,16,4608]{3,2,1,0:T(8,128)(2,1)S(1)}, u32[]{:S(2)}, u32[]{:S(2)}) collective-permute-start(bf16[2,2,16,4608]{3,2,1,0:T(8,128)(2,1)S(1)} %pad_maximum_fusion), channel_id=1, source_target_pairs={{12,0},{13,1},{14,2},{15,3},{8,4},{9,5},{10,6},{11,7},{4,8},{5,9},... | collective-permute-start | bytes 1769480 | tf_op jit(solution)/shard_map/ppermute | solution.py:14
  15.2 1.6 collective-permute-start.2
  16.8 1.7 constant_dynamic-update-slice_fusion.3
  18.5 8.8 %collective-permute-done.6 = bf16[2,2,16,4608]{3,2,1,0:T(8,128)(2,1)S(1)} collective-permute-done((bf16[2,2,16,4608]{3,2,1,0:T(8,128)(2,1)S(1)}, bf16[2,2,16,4608]{3,2,1,0:T(8,128)(2,1)S(1)}, u32[]{:S(2)}, u32[]{:S(2)}) %collective-permute-start.6) | collective-permute-done | bytes 589856 | tf_op jit(solution)/shard_map/ppermute | solution.py:14
  27.5 4.4 %collective-permute-done.1 = bf16[2,2,16,4608]{3,2,1,0:T(8,128)(2,1)S(1)} collective-permute-done((bf16[2,2,16,4608]{3,2,1,0:T(8,128)(2,1)S(1)}, bf16[2,2,16,4608]{3,2,1,0:T(8,128)(2,1)S(1)}, u32[]{:S(2)}, u32[]{:S(2)}) %collective-permute-start.1) | collective-permute-done | bytes 589856 | tf_op jit(solution)/shard_map/ppermute | solution.py:14
  31.9 1.1 collective-permute-start.3
  32.9 0.9 constant_dynamic-update-slice_fusion.2
  33.9 0.9 constant_dynamic-update-slice_fusion.1
  35.5 1.9 %collective-permute-start.9 = (bf16[2,2,16,4608]{3,2,1,0:T(8,128)(2,1)S(1)}, bf16[2,2,16,4608]{3,2,1,0:T(8,128)(2,1)S(1)}, u32[]{:S(2)}, u32[]{:S(2)}) collective-permute-start(bf16[2,2,16,4608]{3,2,1,0:T(8,128)(2,1)S(1)} %collective-permute-done.6), channel_id=1, source_target_pairs={{1,0},{0,1},{3,2},{2,3},{5,4},{4,5},{7,6},{6,7},{9,8},{8,9},{11,10... | collective-permute-start | bytes 1769480 | tf_op jit(solution)/shard_map/ppermute | solution.py:14
  37.5 1.1 slice.231
  38.7 2.6 %collective-permute-start.14 = (bf16[288,1152]{1,0:T(8,128)(2,1)S(1)}, bf16[288,1152]{1,0:T(8,128)(2,1)S(1)}, u32[]{:S(2)}, u32[]{:S(2)}) collective-permute-start(bf16[288,1152]{1,0:T(8,128)(2,1)S(1)} %slice.231), channel_id=1, source_target_pairs={{48,0},{32,16},{16,32},{0,48},{112,64},{96,80},{80,96},{64,112},{4... | collective-permute-start | bytes 1990664 | tf_op jit(solution)/shard_map/ppermute | solution.py:19
  41.3 6.2 %fusion.52.refs_1_ = f32[256,1152]{1,0:T(8,128)S(1)} fusion(bf16[256,4608]{1,0:T(8,128)(2,1)S(1)} %bitcast.189, bf16[4608,1152]{1,0:T(8,128)(2,1)} %param.9), kind=kOutput, calls=%fused_computation.140 | convolution fusion | flops 2717908992 | bytes 14155776 | tf_op jit(solution)/shard_map/dot_general | solution.py:87
  47.8 1.4 slice-done.2
  49.3 3.2 %fusion.53 = f32[256,1152]{1,0:T(8,128)S(1)} fusion(bf16[256,4608]{1,0:T(8,128)(2,1)S(1)} %shard_map.86, bf16[4608,1152]{1,0:T(8,128)(2,1)S(1)} %bitcast.222), kind=kOutput, calls=%fused_computation.141 | convolution fusion | flops 2717908992 | bytes 14155776 | tf_op jit(solution)/shard_map/dot_general | solution.py:91
  53.5 3.4 %collective-permute-start.11 = (bf16[2,2,64,1152]{3,2,1,0:T(8,128)(2,1)S(1)}, bf16[2,2,64,1152]{3,2,1,0:T(8,128)(2,1)S(1)}, u32[]{:S(2)}, u32[]{:S(2)}) collective-permute-start(bf16[2,2,64,1152]{3,2,1,0:T(8,128)(2,1)S(1)} %pad_maximum_fusion.1.refs_1_), channel_id=1, source_target_pairs={{64,0},{80,16},{96,32},{112,48},{0,64},{16,80},{32,96},{48,112},{6... | collective-permute-start | bytes 1769480 | tf_op jit(solution)/shard_map/ppermute | solution.py:19
  57.3 3.2 %fusion = f32[8,2,16,1152]{3,2,1,0:T(8,128)S(1)} fusion(bf16[8,2,16,4608]{3,2,1,0:T(8,128)(2,1)S(1)} %constant_dynamic-update-slice_fusion.5, bf16[4608,1152]{1,0:T(8,128)(2,1)S(1)} %bitcast.222), kind=kOutput, calls=%fused_computation | convolution fusion | flops 2717908992 | bytes 14155776 | tf_op jit(solution)/shard_map/dot_general | solution.py:91
  61.4 3.2 %fusion.2 = f32[8,2,16,1152]{3,2,1,0:T(8,128)S(1)} fusion(bf16[8,2,16,4608]{3,2,1,0:T(8,128)(2,1)S(1)} %constant_dynamic-update-slice_fusion.5, bf16[4608,1152]{1,0:T(8,128)(2,1)S(1)} %bitcast.224), kind=kOutput, calls=%fused_computation.2 | convolution fusion | flops 2717908992 | bytes 14155776 | tf_op jit(solution)/shard_map/dot_general | solution.py:87
  65.4 2.8 %collective-permute-start.16 = (bf16[2,2,64,1152]{3,2,1,0:T(8,128)(2,1)S(1)}, bf16[2,2,64,1152]{3,2,1,0:T(8,128)(2,1)S(1)}, u32[]{:S(2)}, u32[]{:S(2)}) collective-permute-start(bf16[2,2,64,1152]{3,2,1,0:T(8,128)(2,1)S(1)} %pad_maximum_fusion.3), channel_id=1, source_target_pairs={{64,0},{80,16},{96,32},{112,48},{0,64},{16,80},{32,96},{48,112},{6... | collective-permute-start | bytes 1769480 | tf_op jit(solution)/shard_map/ppermute | solution.py:19
  68.2 0.9 fusion.47
  69.1 1.4 collective-permute-done.12.refs_2_
  70.5 6.1 %shard_map.92 = bf16[512,2304]{1,0:T(8,128)(2,1)S(1)} custom-call(bf16[512,1152]{1,0:T(8,128)(2,1)S(1)} %bitcast.186, bf16[576,1152]{1,0:T(8,128)(2,1)S(1)} %shard_map.85.refs_0_, bf16[576,1152]{1,0:T(8,128)(2,1)} %collective-permute-done.4.refs_2_.refs_1_, bf16[288,1152]{1,0:T(8,128)(2,1)S(1)} %collective-permute-done.13.refs_2_, ...), custom_call_target="tpu_custom_call" | custom-call | flops 2717908992 | bytes 7667712 | tf_op jit(solution)/shard_map/pallas_call | solution.py:131
  76.9 1.2 collective-permute-start.15
  78.0 1.6 collective-permute-start.18
  79.9 3.2 %collective-permute-done.16 = bf16[2,2,64,1152]{3,2,1,0:T(8,128)(2,1)S(1)} collective-permute-done((bf16[2,2,64,1152]{3,2,1,0:T(8,128)(2,1)S(1)}, bf16[2,2,64,1152]{3,2,1,0:T(8,128)(2,1)S(1)}, u32[]{:S(2)}, u32[]{:S(2)}) %collective-permute-start.16) | collective-permute-done | bytes 589856 | tf_op jit(solution)/shard_map/ppermute | solution.py:19
  83.2 0.9 fusion.46
  84.6 3.0 %collective-permute-start.19 = (bf16[2,2,16,2304]{3,2,1,0:T(8,128)(2,1)S(1)}, bf16[2,2,16,2304]{3,2,1,0:T(8,128)(2,1)S(1)}, u32[]{:S(2)}, u32[]{:S(2)}) collective-permute-start(bf16[2,2,16,2304]{3,2,1,0:T(8,128)(2,1)S(1)} %get-tuple-element.24), channel_id=1, source_target_pairs={{8,0},{9,1},{10,2},{11,3},{12,4},{13,5},{14,6},{15,7},{0,8},{1,9},... | collective-permute-start | bytes 884744 | tf_op jit(solution)/shard_map/ppermute | solution.py:14
  87.6 0.8 collective-permute-start.21
  88.5 5.6 %collective-permute-done.18.refs_3_.refs_0_ = bf16[2,128,1152]{2,1,0:T(8,128)(2,1)S(1)} collective-permute-done((bf16[2,128,1152]{2,1,0:T(8,128)(2,1)S(1)}, bf16[2,128,1152]{2,1,0:T(8,128)(2,1)S(1)}, u32[]{:S(2)}, u32[]{:S(2)}) %collective-permute-start.18) | collective-permute-done | bytes 589856 | tf_op jit(solution)/shard_map/ppermute | solution.py:19
  94.2 0.8 copy-done.1
  95.0 6.1 %shard_map.94 = bf16[512,2304]{1,0:T(8,128)(2,1)S(1)} custom-call(bf16[512,1152]{1,0:T(8,128)(2,1)S(1)} %bitcast.188, bf16[576,1152]{1,0:T(8,128)(2,1)S(1)} %shard_map.85.refs_0_, bf16[576,1152]{1,0:T(8,128)(2,1)} %collective-permute-done.4.refs_2_.refs_1_, bf16[288,1152]{1,0:T(8,128)(2,1)S(1)} %collective-permute-done.13.refs_2_, ...), custom_call_target="tpu_custom_call" | custom-call | flops 2717908992 | bytes 7667712 | tf_op jit(solution)/shard_map/pallas_call | solution.py:131
  101.3 1.3 collective-permute-start.22
  102.8 1.3 collective-permute-start.24
  104.1 1.0 collective-permute-done.22
  105.6 3.0 %collective-permute-start.25 = (bf16[2,2,16,2304]{3,2,1,0:T(8,128)(2,1)S(1)}, bf16[2,2,16,2304]{3,2,1,0:T(8,128)(2,1)S(1)}, u32[]{:S(2)}, u32[]{:S(2)}) collective-permute-start(bf16[2,2,16,2304]{3,2,1,0:T(8,128)(2,1)S(1)} %get-tuple-element.21), channel_id=1, source_target_pairs={{8,0},{9,1},{10,2},{11,3},{12,4},{13,5},{14,6},{15,7},{0,8},{1,9},... | collective-permute-start | bytes 884744 | tf_op jit(solution)/shard_map/ppermute | solution.py:14
  108.6 0.8 collective-permute-start.27
  109.4 9.7 %collective-permute-done.24.refs_2_ = bf16[2,128,1152]{2,1,0:T(8,128)(2,1)S(1)} collective-permute-done((bf16[2,128,1152]{2,1,0:T(8,128)(2,1)S(1)}, bf16[2,128,1152]{2,1,0:T(8,128)(2,1)S(1)}, u32[]{:S(2)}, u32[]{:S(2)}) %collective-permute-start.24) | collective-permute-done | bytes 589856 | tf_op jit(solution)/shard_map/ppermute | solution.py:19
  119.1 3.3 %collective-permute-done.27 = bf16[2,2,16,2304]{3,2,1,0:T(8,128)(2,1)S(1)} collective-permute-done((bf16[2,2,16,2304]{3,2,1,0:T(8,128)(2,1)S(1)}, bf16[2,2,16,2304]{3,2,1,0:T(8,128)(2,1)S(1)}, u32[]{:S(2)}, u32[]{:S(2)}) %collective-permute-start.27) | collective-permute-done | bytes 294944 | tf_op jit(solution)/shard_map/ppermute | solution.py:14
  122.8 7.6 %collective-permute-done.28 = bf16[2,2,16,2304]{3,2,0,1:T(8,128)(2,1)S(1)} collective-permute-done((bf16[2,2,16,2304]{3,2,0,1:T(8,128)(2,1)S(1)}, bf16[2,2,16,2304]{3,2,0,1:T(8,128)(2,1)S(1)}, u32[]{:S(2)}, u32[]{:S(2)}) %collective-permute-start.28) | collective-permute-done | bytes 294944 | tf_op jit(solution)/shard_map/ppermute | solution.py:14
  130.6 1.3 collective-permute-start.32
  131.9 1.1 collective-permute-start.31
  133.0 0.9 collective-permute-start.30
  134.1 1.1 collective-permute-done.32
  135.2 1.5 collective-permute-done.31
  136.9 0.8 pad_maximum_fusion.4
  137.7 3.2 %collective-permute-start.36 = (bf16[2,2,4,16,576]{4,3,2,1,0:T(8,128)(2,1)S(1)}, bf16[2,2,4,16,576]{4,3,2,1,0:T(8,128)(2,1)}, u32[]{:S(2)}, u32[]{:S(2)}) collective-permute-start(bf16[2,2,4,16,576]{4,3,2,1,0:T(8,128)(2,1)S(1)} %get-tuple-element.40.refs_1_), channel_id=1, source_target_pairs={{12,0},{13,1},{14,2},{15,3},{8,4},{9,5},{10,6},{11,7},{4,8},{5,9},... | collective-permute-start | bytes 884744 | tf_op jit(solution)/shard_map/ppermute | solution.py:14
  141.0 2.9 %collective-permute-start.33 = (bf16[2,2,4,16,576]{4,3,2,1,0:T(8,128)(2,1)S(1)}, bf16[2,2,4,16,576]{4,3,2,1,0:T(8,128)(2,1)S(1)}, u32[]{:S(2)}, u32[]{:S(2)}) collective-permute-start(bf16[2,2,4,16,576]{4,3,2,1,0:T(8,128)(2,1)S(1)} %get-tuple-element.40.refs_1_), channel_id=1, source_target_pairs={{1,0},{0,1},{3,2},{2,3},{5,4},{4,5},{7,6},{6,7},{9,8},{8,9},{11,10... | collective-permute-start | bytes 884744 | tf_op jit(solution)/shard_map/ppermute | solution.py:14
  143.8 2.4 %collective-permute-done.36 = bf16[2,2,4,16,576]{4,3,2,1,0:T(8,128)(2,1)} collective-permute-done((bf16[2,2,4,16,576]{4,3,2,1,0:T(8,128)(2,1)S(1)}, bf16[2,2,4,16,576]{4,3,2,1,0:T(8,128)(2,1)}, u32[]{:S(2)}, u32[]{:S(2)}) %collective-permute-start.36) | collective-permute-done | bytes 294944 | tf_op jit(solution)/shard_map/ppermute | solution.py:14
  146.3 0.9 slice.271
  147.4 0.9 slice.272
  148.3 2.6 %collective-permute-start.38 = (bf16[1,2,4,16,576]{4,3,2,1,0:T(8,128)(2,1)S(1)}, bf16[1,2,4,16,576]{4,3,2,1,0:T(8,128)(2,1)S(1)}, u32[]{:S(2)}, u32[]{:S(2)}) collective-permute-start(bf16[1,2,4,16,576]{4,3,2,1,0:T(8,128)(2,1)S(1)} %slice.272), channel_id=1, source_target_pairs={{12,0},{13,1},{14,2},{15,3},{8,4},{9,5},{10,6},{11,7},{4,8},{5,9},... | collective-permute-start | bytes 442376 | tf_op jit(solution)/shard_map/ppermute | solution.py:14
  151.0 1.2 collective-permute-start.43
  153.1 3.2 %collective-permute-start.34 = (bf16[2,16,2304]{2,1,0:T(8,128)(2,1)S(1)}, bf16[2,16,2304]{2,1,0:T(8,128)(2,1)S(1)}, u32[]{:S(2)}, u32[]{:S(2)}) collective-permute-start(bf16[2,16,2304]{2,1,0:T(8,128)(2,1)S(1)} %shard_map.98), channel_id=1, source_target_pairs={{64,0},{80,16},{96,32},{112,48},{0,64},{16,80},{32,96},{48,112},{6... | collective-permute-start | bytes 442376 | tf_op jit(solution)/shard_map/ppermute | solution.py:19
  156.3 4.6 %collective-permute-start.40 = (bf16[2,2,4,16,576]{4,3,2,1,0:T(8,128)(2,1)}, bf16[2,2,4,16,576]{4,3,2,1,0:T(8,128)(2,1)}, u32[]{:S(2)}, u32[]{:S(2)}) collective-permute-start(bf16[2,2,4,16,576]{4,3,2,1,0:T(8,128)(2,1)} %collective-permute-done.36), channel_id=1, source_target_pairs={{1,0},{0,1},{3,2},{2,3},{5,4},{4,5},{7,6},{6,7},{9,8},{8,9},{11,10... | collective-permute-start | bytes 884744 | tf_op jit(solution)/shard_map/ppermute | solution.py:14
  162.3 1.8 %collective-permute-start.41 = (bf16[2,2,4,16,576]{4,3,2,1,0:T(8,128)(2,1)}, bf16[2,2,4,16,576]{4,3,2,1,0:T(8,128)(2,1)}, u32[]{:S(2)}, u32[]{:S(2)}) collective-permute-start(bf16[2,2,4,16,576]{4,3,2,1,0:T(8,128)(2,1)} %constant_dynamic-update-slice_fusion.12), channel_id=1, source_target_pairs={{1,0},{0,1},{3,2},{2,3},{5,4},{4,5},{7,6},{6,7},{9,8},{8,9},{11,10... | collective-permute-start | bytes 884744 | tf_op jit(solution)/shard_map/ppermute | solution.py:14
  165.1 0.9 concatenate.30
  166.8 1.1 copy-done.6
  167.9 1.0 copy-done.8
  168.9 1.0 copy-done.9
  169.8 7.1 %shard_map.101 = bf16[576,1152]{1,0:T(8,128)(2,1)} custom-call(bf16[256,576]{1,0:T(8,128)(2,1)S(1)} %bitcast.199, bf16[256,576]{1,0:T(8,128)(2,1)} %bitcast.73.refs_1_, bf16[256,576]{1,0:T(8,128)(2,1)} %bitcast.74.refs_2_, bf16[256,576]{1,0:T(8,128)(2,1)} %bitcast.75.refs_3_, bf16[256,576]{1,0:T(8,128)(2,1)S(1)} %bitcast.198, ...), custom_call_target="tpu_custom_call" | custom-call | flops 2717908992 | bytes 8404992 | tf_op jit(solution)/shard_map/pallas_call | solution.py:184
  (156 shorter events, 12.7 us)
Async XLA Ops:
  0.6 1.4 copy-start.11
  0.6 1.4 copy-start.10
  2.0 5.8 %copy-start.12 = (f32[256]{0:T(256)S(1)}, f32[256]{0:T(256)}, u32[]{:S(2)}) copy-start(f32[256]{0:T(256)} %param.8) | copy-start | bytes 3076
  2.1 9.4 %collective-permute-start = (bf16[2,16,4608]{2,1,0:T(8,128)(2,1)S(1)}, bf16[2,16,4608]{2,1,0:T(8,128)(2,1)}, u32[]{:S(2)}, u32[]{:S(2)}) collective-permute-start(bf16[2,16,4608]{2,1,0:T(8,128)(2,1)S(1)} %get-tuple-element.54.refs_1_), channel_id=1, source_target_pairs={{2,0},{3,1},{0,2},{1,3},{6,4},{7,5},{4,6},{5,7},{10,8},{11,9},{8,1... | collective-permute-start | bytes 884744 | tf_op jit(solution)/shard_map/ppermute | solution.py:14
  4.6 30.9 %collective-permute-start.5 = (bf16[576,1152]{1,0:T(8,128)(2,1)S(1)}, bf16[576,1152]{1,0:T(8,128)(2,1)S(1)}, u32[]{:S(2)}, u32[]{:S(2)}) collective-permute-start(bf16[576,1152]{1,0:T(8,128)(2,1)S(1)} %shard_map.85.refs_0_), channel_id=1, source_target_pairs={{48,0},{32,16},{16,32},{0,48},{112,64},{96,80},{80,96},{64,112},{4... | collective-permute-start | bytes 3981320 | tf_op jit(solution)/shard_map/ppermute | solution.py:19
  7.1 30.3 %collective-permute-start.4 = (bf16[576,1152]{1,0:T(8,128)(2,1)S(1)}, bf16[576,1152]{1,0:T(8,128)(2,1)}, u32[]{:S(2)}, u32[]{:S(2)}) collective-permute-start(bf16[576,1152]{1,0:T(8,128)(2,1)S(1)} %shard_map.85.refs_0_), channel_id=1, source_target_pairs={{16,0},{0,16},{48,32},{32,48},{80,64},{64,80},{112,96},{96,112},{1... | collective-permute-start | bytes 3981320 | tf_op jit(solution)/shard_map/ppermute | solution.py:19
  12.5 14.9 %collective-permute-start.6 = (bf16[2,2,16,4608]{3,2,1,0:T(8,128)(2,1)S(1)}, bf16[2,2,16,4608]{3,2,1,0:T(8,128)(2,1)S(1)}, u32[]{:S(2)}, u32[]{:S(2)}) collective-permute-start(bf16[2,2,16,4608]{3,2,1,0:T(8,128)(2,1)S(1)} %pad_maximum_fusion), channel_id=1, source_target_pairs={{12,0},{13,1},{14,2},{15,3},{8,4},{9,5},{10,6},{11,7},{4,8},{5,9},... | collective-permute-start | bytes 1769480 | tf_op jit(solution)/shard_map/ppermute | solution.py:14
  15.2 18.6 %collective-permute-start.2 = (bf16[2,2,16,4608]{3,2,1,0:T(8,128)(2,1)S(1)}, bf16[2,2,16,4608]{3,2,1,0:T(8,128)(2,1)S(1)}, u32[]{:S(2)}, u32[]{:S(2)}) collective-permute-start(bf16[2,2,16,4608]{3,2,1,0:T(8,128)(2,1)S(1)} %pad_maximum_fusion), channel_id=1, source_target_pairs={{1,0},{0,1},{3,2},{2,3},{5,4},{4,5},{7,6},{6,7},{9,8},{8,9},{11,10... | collective-permute-start | bytes 1769480 | tf_op jit(solution)/shard_map/ppermute | solution.py:14
  16.8 15.1 %collective-permute-start.1 = (bf16[2,2,16,4608]{3,2,1,0:T(8,128)(2,1)S(1)}, bf16[2,2,16,4608]{3,2,1,0:T(8,128)(2,1)S(1)}, u32[]{:S(2)}, u32[]{:S(2)}) collective-permute-start(bf16[2,2,16,4608]{3,2,1,0:T(8,128)(2,1)S(1)} %pad_maximum_fusion), channel_id=1, source_target_pairs={{4,0},{5,1},{6,2},{7,3},{0,4},{1,5},{2,6},{3,7},{12,8},{13,9},{14,... | collective-permute-start | bytes 1769480 | tf_op jit(solution)/shard_map/ppermute | solution.py:14
  27.3 20.2 %collective-permute-start.7 = (bf16[1,2,16,4608]{3,2,1,0:T(8,128)(2,1)S(1)}, bf16[1,2,16,4608]{3,2,1,0:T(8,128)(2,1)S(1)}, u32[]{:S(2)}, u32[]{:S(2)}) collective-permute-start(bf16[1,2,16,4608]{3,2,1,0:T(8,128)(2,1)S(1)} %slice.224), channel_id=1, source_target_pairs={{4,0},{5,1},{6,2},{7,3},{0,4},{1,5},{2,6},{3,7},{12,8},{13,9},{14,... | collective-permute-start | bytes 884744 | tf_op jit(solution)/shard_map/ppermute | solution.py:14
  31.9 6.8 %collective-permute-start.3 = (bf16[2,2,16,4608]{3,2,1,0:T(8,128)(2,1)S(1)}, bf16[2,2,16,4608]{3,2,1,0:T(8,128)(2,1)S(1)}, u32[]{:S(2)}, u32[]{:S(2)}) collective-permute-start(bf16[2,2,16,4608]{3,2,1,0:T(8,128)(2,1)S(1)} %collective-permute-done.1), channel_id=1, source_target_pairs={{1,0},{0,1},{3,2},{2,3},{5,4},{4,5},{7,6},{6,7},{9,8},{8,9},{11,10... | collective-permute-start | bytes 1769480 | tf_op jit(solution)/shard_map/ppermute | solution.py:14
  33.8 13.8 %collective-permute-start.8 = (bf16[1,2,16,4608]{3,2,1,0:T(8,128)(2,1)S(1)}, bf16[1,2,16,4608]{3,2,1,0:T(8,128)(2,1)S(1)}, u32[]{:S(2)}, u32[]{:S(2)}) collective-permute-start(bf16[1,2,16,4608]{3,2,1,0:T(8,128)(2,1)S(1)} %slice.225), channel_id=1, source_target_pairs={{12,0},{13,1},{14,2},{15,3},{8,4},{9,5},{10,6},{11,7},{4,8},{5,9},... | collective-permute-start | bytes 884744 | tf_op jit(solution)/shard_map/ppermute | solution.py:14
  34.8 6.5 %copy-start = (bf16[8,2,16,4608]{3,2,1,0:T(8,128)(2,1)S(1)}, bf16[8,2,16,4608]{3,2,1,0:T(8,128)(2,1)}, u32[]{:S(2)}) copy-start(bf16[8,2,16,4608]{3,2,1,0:T(8,128)(2,1)} %constant_dynamic-update-slice_fusion.1) | copy-start | bytes 7077892
  35.5 21.4 %collective-permute-start.9 = (bf16[2,2,16,4608]{3,2,1,0:T(8,128)(2,1)S(1)}, bf16[2,2,16,4608]{3,2,1,0:T(8,128)(2,1)S(1)}, u32[]{:S(2)}, u32[]{:S(2)}) collective-permute-start(bf16[2,2,16,4608]{3,2,1,0:T(8,128)(2,1)S(1)} %collective-permute-done.6), channel_id=1, source_target_pairs={{1,0},{0,1},{3,2},{2,3},{5,4},{4,5},{7,6},{6,7},{9,8},{8,9},{11,10... | collective-permute-start | bytes 1769480 | tf_op jit(solution)/shard_map/ppermute | solution.py:14
  37.4 33.1 %collective-permute-start.13 = (bf16[288,1152]{1,0:T(8,128)(2,1)S(1)}, bf16[288,1152]{1,0:T(8,128)(2,1)S(1)}, u32[]{:S(2)}, u32[]{:S(2)}) collective-permute-start(bf16[288,1152]{1,0:T(8,128)(2,1)S(1)} %slice.230), channel_id=1, source_target_pairs={{16,0},{0,16},{48,32},{32,48},{80,64},{64,80},{112,96},{96,112},{1... | collective-permute-start | bytes 1990664 | tf_op jit(solution)/shard_map/ppermute | solution.py:19
  38.7 31.8 %collective-permute-start.14 = (bf16[288,1152]{1,0:T(8,128)(2,1)S(1)}, bf16[288,1152]{1,0:T(8,128)(2,1)S(1)}, u32[]{:S(2)}, u32[]{:S(2)}) collective-permute-start(bf16[288,1152]{1,0:T(8,128)(2,1)S(1)} %slice.231), channel_id=1, source_target_pairs={{48,0},{32,16},{16,32},{0,48},{112,64},{96,80},{80,96},{64,112},{4... | collective-permute-start | bytes 1990664 | tf_op jit(solution)/shard_map/ppermute | solution.py:19
  41.3 6.5 %slice-start = ((s8[10616832]{0:T(1024)(128)(4,1)}), s8[4194304]{0:T(1024)(128)(4,1)S(1)}, s32[]{:S(2)}) async-start(s8[10616832]{0:T(1024)(128)(4,1)} %bitcast.221), calls=%async_computation | async-start | bytes 8388608
  41.3 6.5 %slice-start.1 = ((s8[10616832]{0:T(1024)(128)(4,1)}), s8[4194304]{0:T(1024)(128)(4,1)S(1)}, s32[]{:S(2)}) async-start(s8[10616832]{0:T(1024)(128)(4,1)} %bitcast.221), calls=%async_computation.1 | async-start | bytes 8388608
  47.6 1.7 slice-start.2
  52.6 4.7 %collective-permute-start.10 = (bf16[2,2,16,4608]{3,2,1,0:T(8,128)(2,1)S(1)}, bf16[2,2,16,4608]{3,2,1,0:T(8,128)(2,1)S(1)}, u32[]{:S(2)}, u32[]{:S(2)}) collective-permute-start(bf16[2,2,16,4608]{3,2,1,0:T(8,128)(2,1)S(1)} %pad_maximum_fusion.2), channel_id=1, source_target_pairs={{1,0},{0,1},{3,2},{2,3},{5,4},{4,5},{7,6},{6,7},{9,8},{8,9},{11,10... | collective-permute-start | bytes 1769480 | tf_op jit(solution)/shard_map/ppermute | solution.py:14
  53.5 17.0 %collective-permute-start.11 = (bf16[2,2,64,1152]{3,2,1,0:T(8,128)(2,1)S(1)}, bf16[2,2,64,1152]{3,2,1,0:T(8,128)(2,1)S(1)}, u32[]{:S(2)}, u32[]{:S(2)}) collective-permute-start(bf16[2,2,64,1152]{3,2,1,0:T(8,128)(2,1)S(1)} %pad_maximum_fusion.1.refs_1_), channel_id=1, source_target_pairs={{64,0},{80,16},{96,32},{112,48},{0,64},{16,80},{32,96},{48,112},{6... | collective-permute-start | bytes 1769480 | tf_op jit(solution)/shard_map/ppermute | solution.py:19
  56.9 13.6 %collective-permute-start.12 = (f32[2,16]{1,0:T(2,128)S(1)}, f32[2,16]{1,0:T(2,128)S(1)}, u32[]{:S(2)}, u32[]{:S(2)}) collective-permute-start(f32[2,16]{1,0:T(2,128)S(1)} %shard_map.90), channel_id=1, source_target_pairs={{64,0},{80,16},{96,32},{112,48},{0,64},{16,80},{32,96},{48,112},{6... | collective-permute-start | bytes 392 | tf_op jit(solution)/shard_map/ppermute | solution.py:19
  57.3 3.3 %slice-start.3 = ((s8[10616832]{0:T(1024)(128)(4,1)}), s8[4194304]{0:T(1024)(128)(4,1)S(1)}, s32[]{:S(2)}) async-start(s8[10616832]{0:T(1024)(128)(4,1)} %bitcast.223), calls=%async_computation.3 | async-start | bytes 8388608
  57.3 3.4 %slice-start.4 = ((s8[10616832]{0:T(1024)(128)(4,1)}), s8[4194304]{0:T(1024)(128)(4,1)S(1)}, s32[]{:S(2)}) async-start(s8[10616832]{0:T(1024)(128)(4,1)} %bitcast.223), calls=%async_computation.4 | async-start | bytes 8388608
  57.3 4.0 %slice-start.5 = ((s8[10616832]{0:T(1024)(128)(4,1)}), s8[2228224]{0:T(1024)(128)(4,1)S(1)}, s32[]{:S(2)}) async-start(s8[10616832]{0:T(1024)(128)(4,1)} %bitcast.223), calls=%async_computation.5 | async-start | bytes 4456448
  65.4 17.7 %collective-permute-start.16 = (bf16[2,2,64,1152]{3,2,1,0:T(8,128)(2,1)S(1)}, bf16[2,2,64,1152]{3,2,1,0:T(8,128)(2,1)S(1)}, u32[]{:S(2)}, u32[]{:S(2)}) collective-permute-start(bf16[2,2,64,1152]{3,2,1,0:T(8,128)(2,1)S(1)} %pad_maximum_fusion.3), channel_id=1, source_target_pairs={{64,0},{80,16},{96,32},{112,48},{0,64},{16,80},{32,96},{48,112},{6... | collective-permute-start | bytes 1769480 | tf_op jit(solution)/shard_map/ppermute | solution.py:19
  76.9 7.2 %collective-permute-start.15 = (bf16[2,4,2,16,2304]{4,3,2,0,1:T(8,128)(2,1)S(1)}, bf16[2,4,2,16,2304]{4,3,2,0,1:T(8,128)(2,1)S(1)}, u32[]{:S(2)}, u32[]{:S(2)}) collective-permute-start(bf16[2,4,2,16,2304]{4,3,2,0,1:T(8,128)(2,1)S(1)} %bitcast.210), channel_id=1, source_target_pairs={{1,0},{0,1},{3,2},{2,3},{5,4},{4,5},{7,6},{6,7},{9,8},{8,9},{11,10... | collective-permute-start | bytes 3538952 | tf_op jit(solution)/shard_map/ppermute | solution.py:14
  78.0 16.1 %collective-permute-start.18 = (bf16[2,128,1152]{2,1,0:T(8,128)(2,1)S(1)}, bf16[2,128,1152]{2,1,0:T(8,128)(2,1)S(1)}, u32[]{:S(2)}, u32[]{:S(2)}) collective-permute-start(bf16[2,128,1152]{2,1,0:T(8,128)(2,1)S(1)} %get-tuple-element.20), channel_id=1, source_target_pairs={{48,0},{32,16},{16,32},{0,48},{112,64},{96,80},{80,96},{64,112},{4... | collective-permute-start | bytes 1769480 | tf_op jit(solution)/shard_map/ppermute | solution.py:19
  79.6 14.6 %collective-permute-start.17 = (bf16[2,128,1152]{2,1,0:T(8,128)(2,1)S(1)}, bf16[2,128,1152]{2,1,0:T(8,128)(2,1)S(1)}, u32[]{:S(2)}, u32[]{:S(2)}) collective-permute-start(bf16[2,128,1152]{2,1,0:T(8,128)(2,1)S(1)} %get-tuple-element.20), channel_id=1, source_target_pairs={{16,0},{0,16},{48,32},{32,48},{80,64},{64,80},{112,96},{96,112},{1... | collective-permute-start | bytes 1769480 | tf_op jit(solution)/shard_map/ppermute | solution.py:19
  84.6 18.1 %collective-permute-start.19 = (bf16[2,2,16,2304]{3,2,1,0:T(8,128)(2,1)S(1)}, bf16[2,2,16,2304]{3,2,1,0:T(8,128)(2,1)S(1)}, u32[]{:S(2)}, u32[]{:S(2)}) collective-permute-start(bf16[2,2,16,2304]{3,2,1,0:T(8,128)(2,1)S(1)} %get-tuple-element.24), channel_id=1, source_target_pairs={{8,0},{9,1},{10,2},{11,3},{12,4},{13,5},{14,6},{15,7},{0,8},{1,9},... | collective-permute-start | bytes 884744 | tf_op jit(solution)/shard_map/ppermute | solution.py:14
  87.6 15.1 %collective-permute-start.21 = (bf16[2,2,16,2304]{3,2,1,0:T(8,128)(2,1)S(1)}, bf16[2,2,16,2304]{3,2,1,0:T(8,128)(2,1)S(1)}, u32[]{:S(2)}, u32[]{:S(2)}) collective-permute-start(bf16[2,2,16,2304]{3,2,1,0:T(8,128)(2,1)S(1)} %get-tuple-element.25), channel_id=1, source_target_pairs={{12,0},{13,1},{14,2},{15,3},{8,4},{9,5},{10,6},{11,7},{4,8},{5,9},... | collective-permute-start | bytes 884744 | tf_op jit(solution)/shard_map/ppermute | solution.py:14
  88.4 14.3 %collective-permute-start.20 = (bf16[2,2,16,2304]{3,2,1,0:T(8,128)(2,1)S(1)}, bf16[2,2,16,2304]{3,2,1,0:T(8,128)(2,1)S(1)}, u32[]{:S(2)}, u32[]{:S(2)}) collective-permute-start(bf16[2,2,16,2304]{3,2,1,0:T(8,128)(2,1)S(1)} %get-tuple-element.26), channel_id=1, source_target_pairs={{4,0},{5,1},{6,2},{7,3},{0,4},{1,5},{2,6},{3,7},{12,8},{13,9},{14,... | collective-permute-start | bytes 884744 | tf_op jit(solution)/shard_map/ppermute | solution.py:14
  94.2 0.8 copy-start.1
  101.3 3.7 %collective-permute-start.22 = (bf16[2,4,2,16,2304]{4,3,2,0,1:T(8,128)(2,1)S(1)}, bf16[2,4,2,16,2304]{4,3,2,0,1:T(8,128)(2,1)S(1)}, u32[]{:S(2)}, u32[]{:S(2)}) collective-permute-start(bf16[2,4,2,16,2304]{4,3,2,0,1:T(8,128)(2,1)S(1)} %bitcast.209), channel_id=1, source_target_pairs={{1,0},{0,1},{3,2},{2,3},{5,4},{4,5},{7,6},{6,7},{9,8},{8,9},{11,10... | collective-permute-start | bytes 3538952 | tf_op jit(solution)/shard_map/ppermute | solution.py:14
  102.8 16.2 %collective-permute-start.24 = (bf16[2,128,1152]{2,1,0:T(8,128)(2,1)S(1)}, bf16[2,128,1152]{2,1,0:T(8,128)(2,1)S(1)}, u32[]{:S(2)}, u32[]{:S(2)}) collective-permute-start(bf16[2,128,1152]{2,1,0:T(8,128)(2,1)S(1)} %shard_map.96), channel_id=1, source_target_pairs={{48,0},{32,16},{16,32},{0,48},{112,64},{96,80},{80,96},{64,112},{4... | collective-permute-start | bytes 1769480 | tf_op jit(solution)/shard_map/ppermute | solution.py:19
  104.1 14.9 %collective-permute-start.23 = (bf16[2,128,1152]{2,1,0:T(8,128)(2,1)S(1)}, bf16[2,128,1152]{2,1,0:T(8,128)(2,1)S(1)}, u32[]{:S(2)}, u32[]{:S(2)}) collective-permute-start(bf16[2,128,1152]{2,1,0:T(8,128)(2,1)S(1)} %shard_map.96), channel_id=1, source_target_pairs={{16,0},{0,16},{48,32},{32,48},{80,64},{64,80},{112,96},{96,112},{1... | collective-permute-start | bytes 1769480 | tf_op jit(solution)/shard_map/ppermute | solution.py:19
  105.6 13.5 %collective-permute-start.25 = (bf16[2,2,16,2304]{3,2,1,0:T(8,128)(2,1)S(1)}, bf16[2,2,16,2304]{3,2,1,0:T(8,128)(2,1)S(1)}, u32[]{:S(2)}, u32[]{:S(2)}) collective-permute-start(bf16[2,2,16,2304]{3,2,1,0:T(8,128)(2,1)S(1)} %get-tuple-element.21), channel_id=1, source_target_pairs={{8,0},{9,1},{10,2},{11,3},{12,4},{13,5},{14,6},{15,7},{0,8},{1,9},... | collective-permute-start | bytes 884744 | tf_op jit(solution)/shard_map/ppermute | solution.py:14
  108.6 13.8 %collective-permute-start.27 = (bf16[2,2,16,2304]{3,2,1,0:T(8,128)(2,1)S(1)}, bf16[2,2,16,2304]{3,2,1,0:T(8,128)(2,1)S(1)}, u32[]{:S(2)}, u32[]{:S(2)}) collective-permute-start(bf16[2,2,16,2304]{3,2,1,0:T(8,128)(2,1)S(1)} %get-tuple-element.22), channel_id=1, source_target_pairs={{12,0},{13,1},{14,2},{15,3},{8,4},{9,5},{10,6},{11,7},{4,8},{5,9},... | collective-permute-start | bytes 884744 | tf_op jit(solution)/shard_map/ppermute | solution.py:14
  109.3 13.1 %collective-permute-start.26 = (bf16[2,2,16,2304]{3,2,1,0:T(8,128)(2,1)S(1)}, bf16[2,2,16,2304]{3,2,1,0:T(8,128)(2,1)S(1)}, u32[]{:S(2)}, u32[]{:S(2)}) collective-permute-start(bf16[2,2,16,2304]{3,2,1,0:T(8,128)(2,1)S(1)} %get-tuple-element.23), channel_id=1, source_target_pairs={{4,0},{5,1},{6,2},{7,3},{0,4},{1,5},{2,6},{3,7},{12,8},{13,9},{14,... | collective-permute-start | bytes 884744 | tf_op jit(solution)/shard_map/ppermute | solution.py:14
  119.1 3.5 %copy-start.5 = (bf16[2,128,1152]{2,1,0:T(8,128)(2,1)}, bf16[2,128,1152]{2,1,0:T(8,128)(2,1)S(1)}, u32[]{:S(2)}) copy-start(bf16[2,128,1152]{2,1,0:T(8,128)(2,1)S(1)} %collective-permute-done.24.refs_2_) | copy-start | bytes 1769476
  122.6 7.7 %collective-permute-start.28 = (bf16[2,2,16,2304]{3,2,0,1:T(8,128)(2,1)S(1)}, bf16[2,2,16,2304]{3,2,0,1:T(8,128)(2,1)S(1)}, u32[]{:S(2)}, u32[]{:S(2)}) collective-permute-start(bf16[2,2,16,2304]{3,2,0,1:T(8,128)(2,1)S(1)} %fusion.23), channel_id=1, source_target_pairs={{2,0},{3,1},{0,2},{1,3},{6,4},{7,5},{4,6},{5,7},{10,8},{11,9},{8,1... | collective-permute-start | bytes 884744 | tf_op jit(solution)/shard_map/ppermute | solution.py:14
  130.6 4.6 %collective-permute-start.32 = (bf16[2,2,16,576]{3,2,0,1:T(8,128)(2,1)S(1)}, bf16[2,2,16,576]{3,2,0,1:T(8,128)(2,1)S(1)}, u32[]{:S(2)}, u32[]{:S(2)}) collective-permute-start(bf16[2,2,16,576]{3,2,0,1:T(8,128)(2,1)S(1)} %get-tuple-element.48), channel_id=1, source_target_pairs={{48,0},{32,16},{16,32},{0,48},{112,64},{96,80},{80,96},{64,112},{4... | collective-permute-start | bytes 221192 | tf_op jit(solution)/shard_map/ppermute | solution.py:19
  131.9 4.8 %collective-permute-start.31 = (bf16[2,2,16,576]{3,2,0,1:T(8,128)(2,1)S(1)}, bf16[2,2,16,576]{3,2,0,1:T(8,128)(2,1)S(1)}, u32[]{:S(2)}, u32[]{:S(2)}) collective-permute-start(bf16[2,2,16,576]{3,2,0,1:T(8,128)(2,1)S(1)} %get-tuple-element.49), channel_id=1, source_target_pairs={{32,0},{48,16},{0,32},{16,48},{96,64},{112,80},{64,96},{80,112},{3... | collective-permute-start | bytes 221192 | tf_op jit(solution)/shard_map/ppermute | solution.py:19
  133.0 3.9 %collective-permute-start.30 = (bf16[2,2,16,576]{3,2,0,1:T(8,128)(2,1)S(1)}, bf16[2,2,16,576]{3,2,0,1:T(8,128)(2,1)S(1)}, u32[]{:S(2)}, u32[]{:S(2)}) collective-permute-start(bf16[2,2,16,576]{3,2,0,1:T(8,128)(2,1)S(1)} %get-tuple-element.50), channel_id=1, source_target_pairs={{16,0},{0,16},{48,32},{32,48},{80,64},{64,80},{112,96},{96,112},{1... | collective-permute-start | bytes 221192 | tf_op jit(solution)/shard_map/ppermute | solution.py:19
  134.0 6.9 %collective-permute-start.29 = (bf16[2,16,2304]{2,1,0:T(8,128)(2,1)S(1)}, bf16[2,16,2304]{2,1,0:T(8,128)(2,1)S(1)}, u32[]{:S(2)}, u32[]{:S(2)}) collective-permute-start(bf16[2,16,2304]{2,1,0:T(8,128)(2,1)S(1)} %fusion.30), channel_id=1, source_target_pairs={{2,0},{3,1},{0,2},{1,3},{6,4},{7,5},{4,6},{5,7},{10,8},{11,9},{8,1... | collective-permute-start | bytes 442376 | tf_op jit(solution)/shard_map/ppermute | solution.py:14
  137.7 8.5 %collective-permute-start.36 = (bf16[2,2,4,16,576]{4,3,2,1,0:T(8,128)(2,1)S(1)}, bf16[2,2,4,16,576]{4,3,2,1,0:T(8,128)(2,1)}, u32[]{:S(2)}, u32[]{:S(2)}) collective-permute-start(bf16[2,2,4,16,576]{4,3,2,1,0:T(8,128)(2,1)S(1)} %get-tuple-element.40.refs_1_), channel_id=1, source_target_pairs={{12,0},{13,1},{14,2},{15,3},{8,4},{9,5},{10,6},{11,7},{4,8},{5,9},... | collective-permute-start | bytes 884744 | tf_op jit(solution)/shard_map/ppermute | solution.py:14
  140.9 6.5 %collective-permute-start.35 = (bf16[2,2,4,16,576]{4,3,2,1,0:T(8,128)(2,1)S(1)}, bf16[2,2,4,16,576]{4,3,2,1,0:T(8,128)(2,1)}, u32[]{:S(2)}, u32[]{:S(2)}) collective-permute-start(bf16[2,2,4,16,576]{4,3,2,1,0:T(8,128)(2,1)S(1)} %get-tuple-element.40.refs_1_), channel_id=1, source_target_pairs={{4,0},{5,1},{6,2},{7,3},{0,4},{1,5},{2,6},{3,7},{12,8},{13,9},{14,... | collective-permute-start | bytes 884744 | tf_op jit(solution)/shard_map/ppermute | solution.py:14
  141.0 11.4 %collective-permute-start.33 = (bf16[2,2,4,16,576]{4,3,2,1,0:T(8,128)(2,1)S(1)}, bf16[2,2,4,16,576]{4,3,2,1,0:T(8,128)(2,1)S(1)}, u32[]{:S(2)}, u32[]{:S(2)}) collective-permute-start(bf16[2,2,4,16,576]{4,3,2,1,0:T(8,128)(2,1)S(1)} %get-tuple-element.40.refs_1_), channel_id=1, source_target_pairs={{1,0},{0,1},{3,2},{2,3},{5,4},{4,5},{7,6},{6,7},{9,8},{8,9},{11,10... | collective-permute-start | bytes 884744 | tf_op jit(solution)/shard_map/ppermute | solution.py:14
  147.2 9.1 %collective-permute-start.37 = (bf16[1,2,4,16,576]{4,3,2,1,0:T(8,128)(2,1)S(1)}, bf16[1,2,4,16,576]{4,3,2,1,0:T(8,128)(2,1)S(1)}, u32[]{:S(2)}, u32[]{:S(2)}) collective-permute-start(bf16[1,2,4,16,576]{4,3,2,1,0:T(8,128)(2,1)S(1)} %slice.271), channel_id=1, source_target_pairs={{4,0},{5,1},{6,2},{7,3},{0,4},{1,5},{2,6},{3,7},{12,8},{13,9},{14,... | collective-permute-start | bytes 442376 | tf_op jit(solution)/shard_map/ppermute | solution.py:14
  148.3 13.3 %collective-permute-start.38 = (bf16[1,2,4,16,576]{4,3,2,1,0:T(8,128)(2,1)S(1)}, bf16[1,2,4,16,576]{4,3,2,1,0:T(8,128)(2,1)S(1)}, u32[]{:S(2)}, u32[]{:S(2)}) collective-permute-start(bf16[1,2,4,16,576]{4,3,2,1,0:T(8,128)(2,1)S(1)} %slice.272), channel_id=1, source_target_pairs={{12,0},{13,1},{14,2},{15,3},{8,4},{9,5},{10,6},{11,7},{4,8},{5,9},... | collective-permute-start | bytes 442376 | tf_op jit(solution)/shard_map/ppermute | solution.py:14
  151.0 15.8 %collective-permute-start.43 = (bf16[2,128,1152]{2,1,0:T(8,128)(2,1)S(1)}, bf16[2,128,1152]{2,1,0:T(8,128)(2,1)}, u32[]{:S(2)}, u32[]{:S(2)}) collective-permute-start(bf16[2,128,1152]{2,1,0:T(8,128)(2,1)S(1)} %shard_map.100), channel_id=1, source_target_pairs={{48,0},{32,16},{16,32},{0,48},{112,64},{96,80},{80,96},{64,112},{4... | collective-permute-start | bytes 1769480 | tf_op jit(solution)/shard_map/ppermute | solution.py:19
  152.2 14.6 %collective-permute-start.42 = (bf16[2,128,1152]{2,1,0:T(8,128)(2,1)S(1)}, bf16[2,128,1152]{2,1,0:T(8,128)(2,1)}, u32[]{:S(2)}, u32[]{:S(2)}) collective-permute-start(bf16[2,128,1152]{2,1,0:T(8,128)(2,1)S(1)} %shard_map.99), channel_id=1, source_target_pairs={{16,0},{0,16},{48,32},{32,48},{80,64},{64,80},{112,96},{96,112},{1... | collective-permute-start | bytes 1769480 | tf_op jit(solution)/shard_map/ppermute | solution.py:19
  152.4 0.7 copy-start.7
  153.1 13.7 %copy-start.2 = (bf16[2,128,1152]{2,1,0:T(8,128)(2,1)S(1)}, bf16[2,128,1152]{2,1,0:T(8,128)(2,1)}, u32[]{:S(2)}) copy-start(bf16[2,128,1152]{2,1,0:T(8,128)(2,1)} %copy-done.1) | copy-start | bytes 1769476
  153.1 13.7 %copy-start.3 = (bf16[1,2,128,1152]{3,2,1,0:T(8,128)(2,1)S(1)}, bf16[1,2,128,1152]{3,2,1,0:T(8,128)(2,1)}, u32[]{:S(2)}) copy-start(bf16[1,2,128,1152]{3,2,1,0:T(8,128)(2,1)} %get-tuple-element.19) | copy-start | bytes 1769476
  153.1 13.7 %copy-start.4 = (bf16[1,2,128,1152]{3,2,1,0:T(8,128)(2,1)S(1)}, bf16[1,2,128,1152]{3,2,1,0:T(8,128)(2,1)}, u32[]{:S(2)}) copy-start(bf16[1,2,128,1152]{3,2,1,0:T(8,128)(2,1)} %get-tuple-element.17) | copy-start | bytes 1769476
  153.1 9.1 %collective-permute-start.34 = (bf16[2,16,2304]{2,1,0:T(8,128)(2,1)S(1)}, bf16[2,16,2304]{2,1,0:T(8,128)(2,1)S(1)}, u32[]{:S(2)}, u32[]{:S(2)}) collective-permute-start(bf16[2,16,2304]{2,1,0:T(8,128)(2,1)S(1)} %shard_map.98), channel_id=1, source_target_pairs={{64,0},{80,16},{96,32},{112,48},{0,64},{16,80},{32,96},{48,112},{6... | collective-permute-start | bytes 442376 | tf_op jit(solution)/shard_map/ppermute | solution.py:19
  156.3 10.5 %collective-permute-start.40 = (bf16[2,2,4,16,576]{4,3,2,1,0:T(8,128)(2,1)}, bf16[2,2,4,16,576]{4,3,2,1,0:T(8,128)(2,1)}, u32[]{:S(2)}, u32[]{:S(2)}) collective-permute-start(bf16[2,2,4,16,576]{4,3,2,1,0:T(8,128)(2,1)} %collective-permute-done.36), channel_id=1, source_target_pairs={{1,0},{0,1},{3,2},{2,3},{5,4},{4,5},{7,6},{6,7},{9,8},{8,9},{11,10... | collective-permute-start | bytes 884744 | tf_op jit(solution)/shard_map/ppermute | solution.py:14
  161.6 5.2 %collective-permute-start.39 = (bf16[2,2,4,16,576]{4,3,2,1,0:T(8,128)(2,1)}, bf16[2,2,4,16,576]{4,3,2,1,0:T(8,128)(2,1)}, u32[]{:S(2)}, u32[]{:S(2)}) collective-permute-start(bf16[2,2,4,16,576]{4,3,2,1,0:T(8,128)(2,1)} %collective-permute-done.35), channel_id=1, source_target_pairs={{1,0},{0,1},{3,2},{2,3},{5,4},{4,5},{7,6},{6,7},{9,8},{8,9},{11,10... | collective-permute-start | bytes 884744 | tf_op jit(solution)/shard_map/ppermute | solution.py:14
  162.3 4.5 %collective-permute-start.41 = (bf16[2,2,4,16,576]{4,3,2,1,0:T(8,128)(2,1)}, bf16[2,2,4,16,576]{4,3,2,1,0:T(8,128)(2,1)}, u32[]{:S(2)}, u32[]{:S(2)}) collective-permute-start(bf16[2,2,4,16,576]{4,3,2,1,0:T(8,128)(2,1)} %constant_dynamic-update-slice_fusion.12), channel_id=1, source_target_pairs={{1,0},{0,1},{3,2},{2,3},{5,4},{4,5},{7,6},{6,7},{9,8},{8,9},{11,10... | collective-permute-start | bytes 884744 | tf_op jit(solution)/shard_map/ppermute | solution.py:14
  166.8 1.1 copy-start.6
  167.9 1.0 copy-start.8
  168.9 1.0 copy-start.9
where the time goes:
time: 178 us; the launch traced here: 177 us
  starting transfers between devices  58.3 us (33%)
  waiting for transfers between devices  54.7 us (31%)
  local copies, waits for them, and re-layouts  21.3 us (12%)
  Pallas kernels  19.2 us (11%)
  matrix products  15.8 us (9%)
  other arithmetic  6.1 us (3%)
    ppermute x27, starting transfers between devices, fetch_t(): return lax.ppermute(value, 'tensor', [(i ^ key, i) for i in range(16)])  35.8 us
    ppermute x27, waiting for transfers between devices, fetch_t(): return lax.ppermute(value, 'tensor', [(i ^ key, i) for i in range(16)])  31.2 us
    ppermute x17, waiting for transfers between devices, fetch_d(): return lax.ppermute(value, 'dp', [(i ^ key, i) for i in range(8)])  23.5 us
    ppermute x17, starting transfers between devices, fetch_d(): return lax.ppermute(value, 'dp', [(i ^ key, i) for i in range(8)])  22.6 us
    unnamed x50, local copies, waits for them, and re-layouts  12.7 us
    pallas_call x2, Pallas kernels, product(): pl.pallas_call(kernel, out_shape=jax.ShapeDtypeStruct((height, columns),...  12.2 us
    dot_general x2, matrix products, gate_of(): jnp.dot(flat, gate_weight, preferred_element_type=jnp.float32)  9.43 us
    pallas_call x1, Pallas kernels, outer_sum(): pl.pallas_call(kernel, out_shape=jax.ShapeDtypeStruct((columns, width), j...  7.07 us
  transfers between devices with their start and end apart: 44, of which 16 were waited for; matrix products, arithmetic and copies ran while one was open for 20% of the time, Pallas kernels for 7%

commit v1 on v0

--- a/solution.py
+++ b/solution.py
@@ -170,11 +170,12 @@
             copy.start()
         for copy in copies:
             copy.wait()
+        turned = weighted_ref[...].T
         for at in range(0, width, tile):
             total = lax.dot_general(
-                weighted_ref[...],
+                turned,
                 hidden_ref[:, :, :, at : at + tile].reshape(tokens, tile),
-                (((0,), (0,)), ((), ())),
+                (((1,), (0,)), ((), ())),
                 preferred_element_type=jnp.float32,
             )
             out_ref[:, at : at + tile] = total.astype(jnp.bfloat16)

time: 178 us -> 178 us (level)
  no operation moved by 1% of the time
where the time goes in v1:
time: 178 us; the launch traced here: 177 us
  starting transfers between devices  58.3 us (33%)
  waiting for transfers between devices  54.7 us (31%)
  local copies, waits for them, and re-layouts  21.3 us (12%)
  Pallas kernels  19.3 us (11%)
  matrix products  15.8 us (9%)
  other arithmetic  6.1 us (3%)
    ppermute x27, starting transfers between devices, fetch_t(): return lax.ppermute(value, 'tensor', [(i ^ key, i) for i in range(16)])  35.8 us
    ppermute x27, waiting for transfers between devices, fetch_t(): return lax.ppermute(value, 'tensor', [(i ^ key, i) for i in range(16)])  31.2 us
    ppermute x17, waiting for transfers between devices, fetch_d(): return lax.ppermute(value, 'dp', [(i ^ key, i) for i in range(8)])  23.5 us
    ppermute x17, starting transfers between devices, fetch_d(): return lax.ppermute(value, 'dp', [(i ^ key, i) for i in range(8)])  22.6 us
    unnamed x50, local copies, waits for them, and re-layouts  12.7 us
    pallas_call x2, Pallas kernels, product(): pl.pallas_call(kernel, out_shape=jax.ShapeDtypeStruct((height, columns),...  12.2 us
    dot_general x2, matrix products, gate_of(): jnp.dot(flat, gate_weight, preferred_element_type=jnp.float32)  9.43 us
    pallas_call x1, Pallas kernels, outer_sum(): pl.pallas_call(kernel, out_shape=jax.ShapeDtypeStruct((columns, width), j...  7.08 us
  transfers between devices with their start and end apart: 44, of which 16 were waited for; matrix products, arithmetic and copies ran while one was open for 20% of the time, Pallas kernels for 7%

profile of v1, /device:TPU:1, one launch (start us, length us, event | category | flops | bytes accessed | tf_op | source)
XLA Modules:
  0.0 177.1 jit_solution(13357644350689899100)
XLA Ops:
  0.7 1.4 copy.149
  2.1 2.5 %collective-permute-start = (bf16[2,16,4608]{2,1,0:T(8,128)(2,1)S(1)}, bf16[2,16,4608]{2,1,0:T(8,128)(2,1)}, u32[]{:S(2)}, u32[]{:S(2)}) collective-permute-start(bf16[2,16,4608]{2,1,0:T(8,128)(2,1)S(1)} %get-tuple-element.54.refs_1_), channel_id=1, source_target_pairs={{2,0},{3,1},{0,2},{1,3},{6,4},{7,5},{4,6},{5,7},{10,8},{11,9},{8,1... | collective-permute-start | bytes 884744 | tf_op jit(solution)/shard_map/ppermute | solution.py:14
  4.6 2.5 %collective-permute-start.5 = (bf16[576,1152]{1,0:T(8,128)(2,1)S(1)}, bf16[576,1152]{1,0:T(8,128)(2,1)S(1)}, u32[]{:S(2)}, u32[]{:S(2)}) collective-permute-start(bf16[576,1152]{1,0:T(8,128)(2,1)S(1)} %shard_map.85.refs_0_), channel_id=1, source_target_pairs={{48,0},{32,16},{16,32},{0,48},{112,64},{96,80},{80,96},{64,112},{4... | collective-permute-start | bytes 3981320 | tf_op jit(solution)/shard_map/ppermute | solution.py:19
  7.9 3.5 %collective-permute-done = bf16[2,16,4608]{2,1,0:T(8,128)(2,1)} collective-permute-done((bf16[2,16,4608]{2,1,0:T(8,128)(2,1)S(1)}, bf16[2,16,4608]{2,1,0:T(8,128)(2,1)}, u32[]{:S(2)}, u32[]{:S(2)}) %collective-permute-start) | collective-permute-done | bytes 294944 | tf_op jit(solution)/shard_map/ppermute | solution.py:14
  11.4 1.0 pad_maximum_fusion
  12.5 2.7 %collective-permute-start.6 = (bf16[2,2,16,4608]{3,2,1,0:T(8,128)(2,1)S(1)}, bf16[2,2,16,4608]{3,2,1,0:T(8,128)(2,1)S(1)}, u32[]{:S(2)}, u32[]{:S(2)}) collective-permute-start(bf16[2,2,16,4608]{3,2,1,0:T(8,128)(2,1)S(1)} %pad_maximum_fusion), channel_id=1, source_target_pairs={{12,0},{13,1},{14,2},{15,3},{8,4},{9,5},{10,6},{11,7},{4,8},{5,9},... | collective-permute-start | bytes 1769480 | tf_op jit(solution)/shard_map/ppermute | solution.py:14
  15.2 1.6 collective-permute-start.2
  16.8 1.7 constant_dynamic-update-slice_fusion.3
  18.5 8.8 %collective-permute-done.6 = bf16[2,2,16,4608]{3,2,1,0:T(8,128)(2,1)S(1)} collective-permute-done((bf16[2,2,16,4608]{3,2,1,0:T(8,128)(2,1)S(1)}, bf16[2,2,16,4608]{3,2,1,0:T(8,128)(2,1)S(1)}, u32[]{:S(2)}, u32[]{:S(2)}) %collective-permute-start.6) | collective-permute-done | bytes 589856 | tf_op jit(solution)/shard_map/ppermute | solution.py:14
  27.5 4.4 %collective-permute-done.1 = bf16[2,2,16,4608]{3,2,1,0:T(8,128)(2,1)S(1)} collective-permute-done((bf16[2,2,16,4608]{3,2,1,0:T(8,128)(2,1)S(1)}, bf16[2,2,16,4608]{3,2,1,0:T(8,128)(2,1)S(1)}, u32[]{:S(2)}, u32[]{:S(2)}) %collective-permute-start.1) | collective-permute-done | bytes 589856 | tf_op jit(solution)/shard_map/ppermute | solution.py:14
  31.9 1.1 collective-permute-start.3
  32.9 0.9 constant_dynamic-update-slice_fusion.2
  33.9 0.9 constant_dynamic-update-slice_fusion.1
  35.5 1.9 %collective-permute-start.9 = (bf16[2,2,16,4608]{3,2,1,0:T(8,128)(2,1)S(1)}, bf16[2,2,16,4608]{3,2,1,0:T(8,128)(2,1)S(1)}, u32[]{:S(2)}, u32[]{:S(2)}) collective-permute-start(bf16[2,2,16,4608]{3,2,1,0:T(8,128)(2,1)S(1)} %collective-permute-done.6), channel_id=1, source_target_pairs={{1,0},{0,1},{3,2},{2,3},{5,4},{4,5},{7,6},{6,7},{9,8},{8,9},{11,10... | collective-permute-start | bytes 1769480 | tf_op jit(solution)/shard_map/ppermute | solution.py:14
  37.5 1.1 slice.231
  38.7 2.6 %collective-permute-start.14 = (bf16[288,1152]{1,0:T(8,128)(2,1)S(1)}, bf16[288,1152]{1,0:T(8,128)(2,1)S(1)}, u32[]{:S(2)}, u32[]{:S(2)}) collective-permute-start(bf16[288,1152]{1,0:T(8,128)(2,1)S(1)} %slice.231), channel_id=1, source_target_pairs={{48,0},{32,16},{16,32},{0,48},{112,64},{96,80},{80,96},{64,112},{4... | collective-permute-start | bytes 1990664 | tf_op jit(solution)/shard_map/ppermute | solution.py:19
  41.3 6.2 %fusion.52.refs_1_ = f32[256,1152]{1,0:T(8,128)S(1)} fusion(bf16[256,4608]{1,0:T(8,128)(2,1)S(1)} %bitcast.189, bf16[4608,1152]{1,0:T(8,128)(2,1)} %param.9), kind=kOutput, calls=%fused_computation.140 | convolution fusion | flops 2717908992 | bytes 14155776 | tf_op jit(solution)/shard_map/dot_general | solution.py:87
  47.8 1.4 slice-done.2
  49.3 3.2 %fusion.53 = f32[256,1152]{1,0:T(8,128)S(1)} fusion(bf16[256,4608]{1,0:T(8,128)(2,1)S(1)} %shard_map.86, bf16[4608,1152]{1,0:T(8,128)(2,1)S(1)} %bitcast.222), kind=kOutput, calls=%fused_computation.141 | convolution fusion | flops 2717908992 | bytes 14155776 | tf_op jit(solution)/shard_map/dot_general | solution.py:91
  53.5 3.4 %collective-permute-start.11 = (bf16[2,2,64,1152]{3,2,1,0:T(8,128)(2,1)S(1)}, bf16[2,2,64,1152]{3,2,1,0:T(8,128)(2,1)S(1)}, u32[]{:S(2)}, u32[]{:S(2)}) collective-permute-start(bf16[2,2,64,1152]{3,2,1,0:T(8,128)(2,1)S(1)} %pad_maximum_fusion.1.refs_1_), channel_id=1, source_target_pairs={{64,0},{80,16},{96,32},{112,48},{0,64},{16,80},{32,96},{48,112},{6... | collective-permute-start | bytes 1769480 | tf_op jit(solution)/shard_map/ppermute | solution.py:19
  57.3 3.2 %fusion = f32[8,2,16,1152]{3,2,1,0:T(8,128)S(1)} fusion(bf16[8,2,16,4608]{3,2,1,0:T(8,128)(2,1)S(1)} %constant_dynamic-update-slice_fusion.5, bf16[4608,1152]{1,0:T(8,128)(2,1)S(1)} %bitcast.222), kind=kOutput, calls=%fused_computation | convolution fusion | flops 2717908992 | bytes 14155776 | tf_op jit(solution)/shard_map/dot_general | solution.py:91
  61.4 3.2 %fusion.2 = f32[8,2,16,1152]{3,2,1,0:T(8,128)S(1)} fusion(bf16[8,2,16,4608]{3,2,1,0:T(8,128)(2,1)S(1)} %constant_dynamic-update-slice_fusion.5, bf16[4608,1152]{1,0:T(8,128)(2,1)S(1)} %bitcast.224), kind=kOutput, calls=%fused_computation.2 | convolution fusion | flops 2717908992 | bytes 14155776 | tf_op jit(solution)/shard_map/dot_general | solution.py:87
  65.4 2.8 %collective-permute-start.16 = (bf16[2,2,64,1152]{3,2,1,0:T(8,128)(2,1)S(1)}, bf16[2,2,64,1152]{3,2,1,0:T(8,128)(2,1)S(1)}, u32[]{:S(2)}, u32[]{:S(2)}) collective-permute-start(bf16[2,2,64,1152]{3,2,1,0:T(8,128)(2,1)S(1)} %pad_maximum_fusion.3), channel_id=1, source_target_pairs={{64,0},{80,16},{96,32},{112,48},{0,64},{16,80},{32,96},{48,112},{6... | collective-permute-start | bytes 1769480 | tf_op jit(solution)/shard_map/ppermute | solution.py:19
  68.2 0.9 fusion.47
  69.1 1.4 collective-permute-done.12.refs_2_
  70.5 6.1 %shard_map.92 = bf16[512,2304]{1,0:T(8,128)(2,1)S(1)} custom-call(bf16[512,1152]{1,0:T(8,128)(2,1)S(1)} %bitcast.186, bf16[576,1152]{1,0:T(8,128)(2,1)S(1)} %shard_map.85.refs_0_, bf16[576,1152]{1,0:T(8,128)(2,1)} %collective-permute-done.4.refs_2_.refs_1_, bf16[288,1152]{1,0:T(8,128)(2,1)S(1)} %collective-permute-done.13.refs_2_, ...), custom_call_target="tpu_custom_call" | custom-call | flops 2717908992 | bytes 7667712 | tf_op jit(solution)/shard_map/pallas_call | solution.py:131
  76.9 1.2 collective-permute-start.15
  78.0 1.6 collective-permute-start.18
  79.9 3.2 %collective-permute-done.16 = bf16[2,2,64,1152]{3,2,1,0:T(8,128)(2,1)S(1)} collective-permute-done((bf16[2,2,64,1152]{3,2,1,0:T(8,128)(2,1)S(1)}, bf16[2,2,64,1152]{3,2,1,0:T(8,128)(2,1)S(1)}, u32[]{:S(2)}, u32[]{:S(2)}) %collective-permute-start.16) | collective-permute-done | bytes 589856 | tf_op jit(solution)/shard_map/ppermute | solution.py:19
  83.2 0.9 fusion.46
  84.6 3.0 %collective-permute-start.19 = (bf16[2,2,16,2304]{3,2,1,0:T(8,128)(2,1)S(1)}, bf16[2,2,16,2304]{3,2,1,0:T(8,128)(2,1)S(1)}, u32[]{:S(2)}, u32[]{:S(2)}) collective-permute-start(bf16[2,2,16,2304]{3,2,1,0:T(8,128)(2,1)S(1)} %get-tuple-element.24), channel_id=1, source_target_pairs={{8,0},{9,1},{10,2},{11,3},{12,4},{13,5},{14,6},{15,7},{0,8},{1,9},... | collective-permute-start | bytes 884744 | tf_op jit(solution)/shard_map/ppermute | solution.py:14
  87.6 0.8 collective-permute-start.21
  88.5 5.6 %collective-permute-done.18.refs_3_.refs_0_ = bf16[2,128,1152]{2,1,0:T(8,128)(2,1)S(1)} collective-permute-done((bf16[2,128,1152]{2,1,0:T(8,128)(2,1)S(1)}, bf16[2,128,1152]{2,1,0:T(8,128)(2,1)S(1)}, u32[]{:S(2)}, u32[]{:S(2)}) %collective-permute-start.18) | collective-permute-done | bytes 589856 | tf_op jit(solution)/shard_map/ppermute | solution.py:19
  94.2 0.8 copy-done.1
  95.0 6.1 %shard_map.94 = bf16[512,2304]{1,0:T(8,128)(2,1)S(1)} custom-call(bf16[512,1152]{1,0:T(8,128)(2,1)S(1)} %bitcast.188, bf16[576,1152]{1,0:T(8,128)(2,1)S(1)} %shard_map.85.refs_0_, bf16[576,1152]{1,0:T(8,128)(2,1)} %collective-permute-done.4.refs_2_.refs_1_, bf16[288,1152]{1,0:T(8,128)(2,1)S(1)} %collective-permute-done.13.refs_2_, ...), custom_call_target="tpu_custom_call" | custom-call | flops 2717908992 | bytes 7667712 | tf_op jit(solution)/shard_map/pallas_call | solution.py:131
  101.3 1.3 collective-permute-start.22
  102.8 1.3 collective-permute-start.24
  104.1 1.0 collective-permute-done.22
  105.6 3.0 %collective-permute-start.25 = (bf16[2,2,16,2304]{3,2,1,0:T(8,128)(2,1)S(1)}, bf16[2,2,16,2304]{3,2,1,0:T(8,128)(2,1)S(1)}, u32[]{:S(2)}, u32[]{:S(2)}) collective-permute-start(bf16[2,2,16,2304]{3,2,1,0:T(8,128)(2,1)S(1)} %get-tuple-element.21), channel_id=1, source_target_pairs={{8,0},{9,1},{10,2},{11,3},{12,4},{13,5},{14,6},{15,7},{0,8},{1,9},... | collective-permute-start | bytes 884744 | tf_op jit(solution)/shard_map/ppermute | solution.py:14
  108.6 0.8 collective-permute-start.27
  109.4 9.7 %collective-permute-done.24.refs_2_ = bf16[2,128,1152]{2,1,0:T(8,128)(2,1)S(1)} collective-permute-done((bf16[2,128,1152]{2,1,0:T(8,128)(2,1)S(1)}, bf16[2,128,1152]{2,1,0:T(8,128)(2,1)S(1)}, u32[]{:S(2)}, u32[]{:S(2)}) %collective-permute-start.24) | collective-permute-done | bytes 589856 | tf_op jit(solution)/shard_map/ppermute | solution.py:19
  119.1 3.3 %collective-permute-done.27 = bf16[2,2,16,2304]{3,2,1,0:T(8,128)(2,1)S(1)} collective-permute-done((bf16[2,2,16,2304]{3,2,1,0:T(8,128)(2,1)S(1)}, bf16[2,2,16,2304]{3,2,1,0:T(8,128)(2,1)S(1)}, u32[]{:S(2)}, u32[]{:S(2)}) %collective-permute-start.27) | collective-permute-done | bytes 294944 | tf_op jit(solution)/shard_map/ppermute | solution.py:14
  122.8 7.6 %collective-permute-done.28 = bf16[2,2,16,2304]{3,2,0,1:T(8,128)(2,1)S(1)} collective-permute-done((bf16[2,2,16,2304]{3,2,0,1:T(8,128)(2,1)S(1)}, bf16[2,2,16,2304]{3,2,0,1:T(8,128)(2,1)S(1)}, u32[]{:S(2)}, u32[]{:S(2)}) %collective-permute-start.28) | collective-permute-done | bytes 294944 | tf_op jit(solution)/shard_map/ppermute | solution.py:14
  130.6 1.3 collective-permute-start.32
  131.9 1.1 collective-permute-start.31
  133.0 0.9 collective-permute-start.30
  134.1 1.1 collective-permute-done.32
  135.2 1.5 collective-permute-done.31
  136.9 0.8 pad_maximum_fusion.4
  137.7 3.2 %collective-permute-start.36 = (bf16[2,2,4,16,576]{4,3,2,1,0:T(8,128)(2,1)S(1)}, bf16[2,2,4,16,576]{4,3,2,1,0:T(8,128)(2,1)}, u32[]{:S(2)}, u32[]{:S(2)}) collective-permute-start(bf16[2,2,4,16,576]{4,3,2,1,0:T(8,128)(2,1)S(1)} %get-tuple-element.40.refs_1_), channel_id=1, source_target_pairs={{12,0},{13,1},{14,2},{15,3},{8,4},{9,5},{10,6},{11,7},{4,8},{5,9},... | collective-permute-start | bytes 884744 | tf_op jit(solution)/shard_map/ppermute | solution.py:14
  141.0 2.9 %collective-permute-start.33 = (bf16[2,2,4,16,576]{4,3,2,1,0:T(8,128)(2,1)S(1)}, bf16[2,2,4,16,576]{4,3,2,1,0:T(8,128)(2,1)S(1)}, u32[]{:S(2)}, u32[]{:S(2)}) collective-permute-start(bf16[2,2,4,16,576]{4,3,2,1,0:T(8,128)(2,1)S(1)} %get-tuple-element.40.refs_1_), channel_id=1, source_target_pairs={{1,0},{0,1},{3,2},{2,3},{5,4},{4,5},{7,6},{6,7},{9,8},{8,9},{11,10... | collective-permute-start | bytes 884744 | tf_op jit(solution)/shard_map/ppermute | solution.py:14
  143.8 2.4 %collective-permute-done.36 = bf16[2,2,4,16,576]{4,3,2,1,0:T(8,128)(2,1)} collective-permute-done((bf16[2,2,4,16,576]{4,3,2,1,0:T(8,128)(2,1)S(1)}, bf16[2,2,4,16,576]{4,3,2,1,0:T(8,128)(2,1)}, u32[]{:S(2)}, u32[]{:S(2)}) %collective-permute-start.36) | collective-permute-done | bytes 294944 | tf_op jit(solution)/shard_map/ppermute | solution.py:14
  146.3 0.9 slice.271
  147.4 0.9 slice.272
  148.3 2.6 %collective-permute-start.38 = (bf16[1,2,4,16,576]{4,3,2,1,0:T(8,128)(2,1)S(1)}, bf16[1,2,4,16,576]{4,3,2,1,0:T(8,128)(2,1)S(1)}, u32[]{:S(2)}, u32[]{:S(2)}) collective-permute-start(bf16[1,2,4,16,576]{4,3,2,1,0:T(8,128)(2,1)S(1)} %slice.272), channel_id=1, source_target_pairs={{12,0},{13,1},{14,2},{15,3},{8,4},{9,5},{10,6},{11,7},{4,8},{5,9},... | collective-permute-start | bytes 442376 | tf_op jit(solution)/shard_map/ppermute | solution.py:14
  151.0 1.2 collective-permute-start.43
  153.1 3.2 %collective-permute-start.34 = (bf16[2,16,2304]{2,1,0:T(8,128)(2,1)S(1)}, bf16[2,16,2304]{2,1,0:T(8,128)(2,1)S(1)}, u32[]{:S(2)}, u32[]{:S(2)}) collective-permute-start(bf16[2,16,2304]{2,1,0:T(8,128)(2,1)S(1)} %shard_map.98), channel_id=1, source_target_pairs={{64,0},{80,16},{96,32},{112,48},{0,64},{16,80},{32,96},{48,112},{6... | collective-permute-start | bytes 442376 | tf_op jit(solution)/shard_map/ppermute | solution.py:19
  156.3 4.6 %collective-permute-start.40 = (bf16[2,2,4,16,576]{4,3,2,1,0:T(8,128)(2,1)}, bf16[2,2,4,16,576]{4,3,2,1,0:T(8,128)(2,1)}, u32[]{:S(2)}, u32[]{:S(2)}) collective-permute-start(bf16[2,2,4,16,576]{4,3,2,1,0:T(8,128)(2,1)} %collective-permute-done.36), channel_id=1, source_target_pairs={{1,0},{0,1},{3,2},{2,3},{5,4},{4,5},{7,6},{6,7},{9,8},{8,9},{11,10... | collective-permute-start | bytes 884744 | tf_op jit(solution)/shard_map/ppermute | solution.py:14
  162.3 1.8 %collective-permute-start.41 = (bf16[2,2,4,16,576]{4,3,2,1,0:T(8,128)(2,1)}, bf16[2,2,4,16,576]{4,3,2,1,0:T(8,128)(2,1)}, u32[]{:S(2)}, u32[]{:S(2)}) collective-permute-start(bf16[2,2,4,16,576]{4,3,2,1,0:T(8,128)(2,1)} %constant_dynamic-update-slice_fusion.12), channel_id=1, source_target_pairs={{1,0},{0,1},{3,2},{2,3},{5,4},{4,5},{7,6},{6,7},{9,8},{8,9},{11,10... | collective-permute-start | bytes 884744 | tf_op jit(solution)/shard_map/ppermute | solution.py:14
  165.1 0.9 concatenate.30
  166.8 1.1 copy-done.6
  167.9 1.0 copy-done.8
  168.9 1.0 copy-done.9
  169.8 7.1 %shard_map.101 = bf16[576,1152]{1,0:T(8,128)(2,1)} custom-call(bf16[256,576]{1,0:T(8,128)(2,1)S(1)} %bitcast.199, bf16[256,576]{1,0:T(8,128)(2,1)} %bitcast.73.refs_1_, bf16[256,576]{1,0:T(8,128)(2,1)} %bitcast.74.refs_2_, bf16[256,576]{1,0:T(8,128)(2,1)} %bitcast.75.refs_3_, bf16[256,576]{1,0:T(8,128)(2,1)S(1)} %bitcast.198, ...), custom_call_target="tpu_custom_call" | custom-call | flops 2717908992 | bytes 8404992 | tf_op jit(solution)/shard_map/pallas_call | solution.py:185
  (156 shorter events, 12.7 us)
Async XLA Ops:
  0.6 1.4 copy-start.11
  0.6 1.4 copy-start.10
  2.0 5.8 %copy-start.12 = (f32[256]{0:T(256)S(1)}, f32[256]{0:T(256)}, u32[]{:S(2)}) copy-start(f32[256]{0:T(256)} %param.8) | copy-start | bytes 3076
  2.1 9.4 %collective-permute-start = (bf16[2,16,4608]{2,1,0:T(8,128)(2,1)S(1)}, bf16[2,16,4608]{2,1,0:T(8,128)(2,1)}, u32[]{:S(2)}, u32[]{:S(2)}) collective-permute-start(bf16[2,16,4608]{2,1,0:T(8,128)(2,1)S(1)} %get-tuple-element.54.refs_1_), channel_id=1, source_target_pairs={{2,0},{3,1},{0,2},{1,3},{6,4},{7,5},{4,6},{5,7},{10,8},{11,9},{8,1... | collective-permute-start | bytes 884744 | tf_op jit(solution)/shard_map/ppermute | solution.py:14
  4.6 30.9 %collective-permute-start.5 = (bf16[576,1152]{1,0:T(8,128)(2,1)S(1)}, bf16[576,1152]{1,0:T(8,128)(2,1)S(1)}, u32[]{:S(2)}, u32[]{:S(2)}) collective-permute-start(bf16[576,1152]{1,0:T(8,128)(2,1)S(1)} %shard_map.85.refs_0_), channel_id=1, source_target_pairs={{48,0},{32,16},{16,32},{0,48},{112,64},{96,80},{80,96},{64,112},{4... | collective-permute-start | bytes 3981320 | tf_op jit(solution)/shard_map/ppermute | solution.py:19
  7.1 30.3 %collective-permute-start.4 = (bf16[576,1152]{1,0:T(8,128)(2,1)S(1)}, bf16[576,1152]{1,0:T(8,128)(2,1)}, u32[]{:S(2)}, u32[]{:S(2)}) collective-permute-start(bf16[576,1152]{1,0:T(8,128)(2,1)S(1)} %shard_map.85.refs_0_), channel_id=1, source_target_pairs={{16,0},{0,16},{48,32},{32,48},{80,64},{64,80},{112,96},{96,112},{1... | collective-permute-start | bytes 3981320 | tf_op jit(solution)/shard_map/ppermute | solution.py:19
  12.5 14.9 %collective-permute-start.6 = (bf16[2,2,16,4608]{3,2,1,0:T(8,128)(2,1)S(1)}, bf16[2,2,16,4608]{3,2,1,0:T(8,128)(2,1)S(1)}, u32[]{:S(2)}, u32[]{:S(2)}) collective-permute-start(bf16[2,2,16,4608]{3,2,1,0:T(8,128)(2,1)S(1)} %pad_maximum_fusion), channel_id=1, source_target_pairs={{12,0},{13,1},{14,2},{15,3},{8,4},{9,5},{10,6},{11,7},{4,8},{5,9},... | collective-permute-start | bytes 1769480 | tf_op jit(solution)/shard_map/ppermute | solution.py:14
  15.2 18.6 %collective-permute-start.2 = (bf16[2,2,16,4608]{3,2,1,0:T(8,128)(2,1)S(1)}, bf16[2,2,16,4608]{3,2,1,0:T(8,128)(2,1)S(1)}, u32[]{:S(2)}, u32[]{:S(2)}) collective-permute-start(bf16[2,2,16,4608]{3,2,1,0:T(8,128)(2,1)S(1)} %pad_maximum_fusion), channel_id=1, source_target_pairs={{1,0},{0,1},{3,2},{2,3},{5,4},{4,5},{7,6},{6,7},{9,8},{8,9},{11,10... | collective-permute-start | bytes 1769480 | tf_op jit(solution)/shard_map/ppermute | solution.py:14
  16.8 15.1 %collective-permute-start.1 = (bf16[2,2,16,4608]{3,2,1,0:T(8,128)(2,1)S(1)}, bf16[2,2,16,4608]{3,2,1,0:T(8,128)(2,1)S(1)}, u32[]{:S(2)}, u32[]{:S(2)}) collective-permute-start(bf16[2,2,16,4608]{3,2,1,0:T(8,128)(2,1)S(1)} %pad_maximum_fusion), channel_id=1, source_target_pairs={{4,0},{5,1},{6,2},{7,3},{0,4},{1,5},{2,6},{3,7},{12,8},{13,9},{14,... | collective-permute-start | bytes 1769480 | tf_op jit(solution)/shard_map/ppermute | solution.py:14
  27.3 20.2 %collective-permute-start.7 = (bf16[1,2,16,4608]{3,2,1,0:T(8,128)(2,1)S(1)}, bf16[1,2,16,4608]{3,2,1,0:T(8,128)(2,1)S(1)}, u32[]{:S(2)}, u32[]{:S(2)}) collective-permute-start(bf16[1,2,16,4608]{3,2,1,0:T(8,128)(2,1)S(1)} %slice.224), channel_id=1, source_target_pairs={{4,0},{5,1},{6,2},{7,3},{0,4},{1,5},{2,6},{3,7},{12,8},{13,9},{14,... | collective-permute-start | bytes 884744 | tf_op jit(solution)/shard_map/ppermute | solution.py:14
  31.9 6.8 %collective-permute-start.3 = (bf16[2,2,16,4608]{3,2,1,0:T(8,128)(2,1)S(1)}, bf16[2,2,16,4608]{3,2,1,0:T(8,128)(2,1)S(1)}, u32[]{:S(2)}, u32[]{:S(2)}) collective-permute-start(bf16[2,2,16,4608]{3,2,1,0:T(8,128)(2,1)S(1)} %collective-permute-done.1), channel_id=1, source_target_pairs={{1,0},{0,1},{3,2},{2,3},{5,4},{4,5},{7,6},{6,7},{9,8},{8,9},{11,10... | collective-permute-start | bytes 1769480 | tf_op jit(solution)/shard_map/ppermute | solution.py:14
  33.8 13.8 %collective-permute-start.8 = (bf16[1,2,16,4608]{3,2,1,0:T(8,128)(2,1)S(1)}, bf16[1,2,16,4608]{3,2,1,0:T(8,128)(2,1)S(1)}, u32[]{:S(2)}, u32[]{:S(2)}) collective-permute-start(bf16[1,2,16,4608]{3,2,1,0:T(8,128)(2,1)S(1)} %slice.225), channel_id=1, source_target_pairs={{12,0},{13,1},{14,2},{15,3},{8,4},{9,5},{10,6},{11,7},{4,8},{5,9},... | collective-permute-start | bytes 884744 | tf_op jit(solution)/shard_map/ppermute | solution.py:14
  34.8 6.5 %copy-start = (bf16[8,2,16,4608]{3,2,1,0:T(8,128)(2,1)S(1)}, bf16[8,2,16,4608]{3,2,1,0:T(8,128)(2,1)}, u32[]{:S(2)}) copy-start(bf16[8,2,16,4608]{3,2,1,0:T(8,128)(2,1)} %constant_dynamic-update-slice_fusion.1) | copy-start | bytes 7077892
  35.5 21.4 %collective-permute-start.9 = (bf16[2,2,16,4608]{3,2,1,0:T(8,128)(2,1)S(1)}, bf16[2,2,16,4608]{3,2,1,0:T(8,128)(2,1)S(1)}, u32[]{:S(2)}, u32[]{:S(2)}) collective-permute-start(bf16[2,2,16,4608]{3,2,1,0:T(8,128)(2,1)S(1)} %collective-permute-done.6), channel_id=1, source_target_pairs={{1,0},{0,1},{3,2},{2,3},{5,4},{4,5},{7,6},{6,7},{9,8},{8,9},{11,10... | collective-permute-start | bytes 1769480 | tf_op jit(solution)/shard_map/ppermute | solution.py:14
  37.4 33.1 %collective-permute-start.13 = (bf16[288,1152]{1,0:T(8,128)(2,1)S(1)}, bf16[288,1152]{1,0:T(8,128)(2,1)S(1)}, u32[]{:S(2)}, u32[]{:S(2)}) collective-permute-start(bf16[288,1152]{1,0:T(8,128)(2,1)S(1)} %slice.230), channel_id=1, source_target_pairs={{16,0},{0,16},{48,32},{32,48},{80,64},{64,80},{112,96},{96,112},{1... | collective-permute-start | bytes 1990664 | tf_op jit(solution)/shard_map/ppermute | solution.py:19
  38.7 31.8 %collective-permute-start.14 = (bf16[288,1152]{1,0:T(8,128)(2,1)S(1)}, bf16[288,1152]{1,0:T(8,128)(2,1)S(1)}, u32[]{:S(2)}, u32[]{:S(2)}) collective-permute-start(bf16[288,1152]{1,0:T(8,128)(2,1)S(1)} %slice.231), channel_id=1, source_target_pairs={{48,0},{32,16},{16,32},{0,48},{112,64},{96,80},{80,96},{64,112},{4... | collective-permute-start | bytes 1990664 | tf_op jit(solution)/shard_map/ppermute | solution.py:19
  41.3 6.5 %slice-start = ((s8[10616832]{0:T(1024)(128)(4,1)}), s8[4194304]{0:T(1024)(128)(4,1)S(1)}, s32[]{:S(2)}) async-start(s8[10616832]{0:T(1024)(128)(4,1)} %bitcast.221), calls=%async_computation | async-start | bytes 8388608
  41.3 6.5 %slice-start.1 = ((s8[10616832]{0:T(1024)(128)(4,1)}), s8[4194304]{0:T(1024)(128)(4,1)S(1)}, s32[]{:S(2)}) async-start(s8[10616832]{0:T(1024)(128)(4,1)} %bitcast.221), calls=%async_computation.1 | async-start | bytes 8388608
  47.6 1.7 slice-start.2
  52.6 4.7 %collective-permute-start.10 = (bf16[2,2,16,4608]{3,2,1,0:T(8,128)(2,1)S(1)}, bf16[2,2,16,4608]{3,2,1,0:T(8,128)(2,1)S(1)}, u32[]{:S(2)}, u32[]{:S(2)}) collective-permute-start(bf16[2,2,16,4608]{3,2,1,0:T(8,128)(2,1)S(1)} %pad_maximum_fusion.2), channel_id=1, source_target_pairs={{1,0},{0,1},{3,2},{2,3},{5,4},{4,5},{7,6},{6,7},{9,8},{8,9},{11,10... | collective-permute-start | bytes 1769480 | tf_op jit(solution)/shard_map/ppermute | solution.py:14
  53.5 17.0 %collective-permute-start.11 = (bf16[2,2,64,1152]{3,2,1,0:T(8,128)(2,1)S(1)}, bf16[2,2,64,1152]{3,2,1,0:T(8,128)(2,1)S(1)}, u32[]{:S(2)}, u32[]{:S(2)}) collective-permute-start(bf16[2,2,64,1152]{3,2,1,0:T(8,128)(2,1)S(1)} %pad_maximum_fusion.1.refs_1_), channel_id=1, source_target_pairs={{64,0},{80,16},{96,32},{112,48},{0,64},{16,80},{32,96},{48,112},{6... | collective-permute-start | bytes 1769480 | tf_op jit(solution)/shard_map/ppermute | solution.py:19
  56.9 13.6 %collective-permute-start.12 = (f32[2,16]{1,0:T(2,128)S(1)}, f32[2,16]{1,0:T(2,128)S(1)}, u32[]{:S(2)}, u32[]{:S(2)}) collective-permute-start(f32[2,16]{1,0:T(2,128)S(1)} %shard_map.90), channel_id=1, source_target_pairs={{64,0},{80,16},{96,32},{112,48},{0,64},{16,80},{32,96},{48,112},{6... | collective-permute-start | bytes 392 | tf_op jit(solution)/shard_map/ppermute | solution.py:19
  57.3 3.3 %slice-start.3 = ((s8[10616832]{0:T(1024)(128)(4,1)}), s8[4194304]{0:T(1024)(128)(4,1)S(1)}, s32[]{:S(2)}) async-start(s8[10616832]{0:T(1024)(128)(4,1)} %bitcast.223), calls=%async_computation.3 | async-start | bytes 8388608
  57.3 3.4 %slice-start.4 = ((s8[10616832]{0:T(1024)(128)(4,1)}), s8[4194304]{0:T(1024)(128)(4,1)S(1)}, s32[]{:S(2)}) async-start(s8[10616832]{0:T(1024)(128)(4,1)} %bitcast.223), calls=%async_computation.4 | async-start | bytes 8388608
  57.3 4.0 %slice-start.5 = ((s8[10616832]{0:T(1024)(128)(4,1)}), s8[2228224]{0:T(1024)(128)(4,1)S(1)}, s32[]{:S(2)}) async-start(s8[10616832]{0:T(1024)(128)(4,1)} %bitcast.223), calls=%async_computation.5 | async-start | bytes 4456448
  65.4 17.7 %collective-permute-start.16 = (bf16[2,2,64,1152]{3,2,1,0:T(8,128)(2,1)S(1)}, bf16[2,2,64,1152]{3,2,1,0:T(8,128)(2,1)S(1)}, u32[]{:S(2)}, u32[]{:S(2)}) collective-permute-start(bf16[2,2,64,1152]{3,2,1,0:T(8,128)(2,1)S(1)} %pad_maximum_fusion.3), channel_id=1, source_target_pairs={{64,0},{80,16},{96,32},{112,48},{0,64},{16,80},{32,96},{48,112},{6... | collective-permute-start | bytes 1769480 | tf_op jit(solution)/shard_map/ppermute | solution.py:19
  76.9 7.2 %collective-permute-start.15 = (bf16[2,4,2,16,2304]{4,3,2,0,1:T(8,128)(2,1)S(1)}, bf16[2,4,2,16,2304]{4,3,2,0,1:T(8,128)(2,1)S(1)}, u32[]{:S(2)}, u32[]{:S(2)}) collective-permute-start(bf16[2,4,2,16,2304]{4,3,2,0,1:T(8,128)(2,1)S(1)} %bitcast.210), channel_id=1, source_target_pairs={{1,0},{0,1},{3,2},{2,3},{5,4},{4,5},{7,6},{6,7},{9,8},{8,9},{11,10... | collective-permute-start | bytes 3538952 | tf_op jit(solution)/shard_map/ppermute | solution.py:14
  78.0 16.1 %collective-permute-start.18 = (bf16[2,128,1152]{2,1,0:T(8,128)(2,1)S(1)}, bf16[2,128,1152]{2,1,0:T(8,128)(2,1)S(1)}, u32[]{:S(2)}, u32[]{:S(2)}) collective-permute-start(bf16[2,128,1152]{2,1,0:T(8,128)(2,1)S(1)} %get-tuple-element.20), channel_id=1, source_target_pairs={{48,0},{32,16},{16,32},{0,48},{112,64},{96,80},{80,96},{64,112},{4... | collective-permute-start | bytes 1769480 | tf_op jit(solution)/shard_map/ppermute | solution.py:19
  79.6 14.6 %collective-permute-start.17 = (bf16[2,128,1152]{2,1,0:T(8,128)(2,1)S(1)}, bf16[2,128,1152]{2,1,0:T(8,128)(2,1)S(1)}, u32[]{:S(2)}, u32[]{:S(2)}) collective-permute-start(bf16[2,128,1152]{2,1,0:T(8,128)(2,1)S(1)} %get-tuple-element.20), channel_id=1, source_target_pairs={{16,0},{0,16},{48,32},{32,48},{80,64},{64,80},{112,96},{96,112},{1... | collective-permute-start | bytes 1769480 | tf_op jit(solution)/shard_map/ppermute | solution.py:19
  84.6 18.1 %collective-permute-start.19 = (bf16[2,2,16,2304]{3,2,1,0:T(8,128)(2,1)S(1)}, bf16[2,2,16,2304]{3,2,1,0:T(8,128)(2,1)S(1)}, u32[]{:S(2)}, u32[]{:S(2)}) collective-permute-start(bf16[2,2,16,2304]{3,2,1,0:T(8,128)(2,1)S(1)} %get-tuple-element.24), channel_id=1, source_target_pairs={{8,0},{9,1},{10,2},{11,3},{12,4},{13,5},{14,6},{15,7},{0,8},{1,9},... | collective-permute-start | bytes 884744 | tf_op jit(solution)/shard_map/ppermute | solution.py:14
  87.6 15.1 %collective-permute-start.21 = (bf16[2,2,16,2304]{3,2,1,0:T(8,128)(2,1)S(1)}, bf16[2,2,16,2304]{3,2,1,0:T(8,128)(2,1)S(1)}, u32[]{:S(2)}, u32[]{:S(2)}) collective-permute-start(bf16[2,2,16,2304]{3,2,1,0:T(8,128)(2,1)S(1)} %get-tuple-element.25), channel_id=1, source_target_pairs={{12,0},{13,1},{14,2},{15,3},{8,4},{9,5},{10,6},{11,7},{4,8},{5,9},... | collective-permute-start | bytes 884744 | tf_op jit(solution)/shard_map/ppermute | solution.py:14
  88.4 14.3 %collective-permute-start.20 = (bf16[2,2,16,2304]{3,2,1,0:T(8,128)(2,1)S(1)}, bf16[2,2,16,2304]{3,2,1,0:T(8,128)(2,1)S(1)}, u32[]{:S(2)}, u32[]{:S(2)}) collective-permute-start(bf16[2,2,16,2304]{3,2,1,0:T(8,128)(2,1)S(1)} %get-tuple-element.26), channel_id=1, source_target_pairs={{4,0},{5,1},{6,2},{7,3},{0,4},{1,5},{2,6},{3,7},{12,8},{13,9},{14,... | collective-permute-start | bytes 884744 | tf_op jit(solution)/shard_map/ppermute | solution.py:14
  94.2 0.8 copy-start.1
  101.3 3.7 %collective-permute-start.22 = (bf16[2,4,2,16,2304]{4,3,2,0,1:T(8,128)(2,1)S(1)}, bf16[2,4,2,16,2304]{4,3,2,0,1:T(8,128)(2,1)S(1)}, u32[]{:S(2)}, u32[]{:S(2)}) collective-permute-start(bf16[2,4,2,16,2304]{4,3,2,0,1:T(8,128)(2,1)S(1)} %bitcast.209), channel_id=1, source_target_pairs={{1,0},{0,1},{3,2},{2,3},{5,4},{4,5},{7,6},{6,7},{9,8},{8,9},{11,10... | collective-permute-start | bytes 3538952 | tf_op jit(solution)/shard_map/ppermute | solution.py:14
  102.8 16.2 %collective-permute-start.24 = (bf16[2,128,1152]{2,1,0:T(8,128)(2,1)S(1)}, bf16[2,128,1152]{2,1,0:T(8,128)(2,1)S(1)}, u32[]{:S(2)}, u32[]{:S(2)}) collective-permute-start(bf16[2,128,1152]{2,1,0:T(8,128)(2,1)S(1)} %shard_map.96), channel_id=1, source_target_pairs={{48,0},{32,16},{16,32},{0,48},{112,64},{96,80},{80,96},{64,112},{4... | collective-permute-start | bytes 1769480 | tf_op jit(solution)/shard_map/ppermute | solution.py:19
  104.1 14.9 %collective-permute-start.23 = (bf16[2,128,1152]{2,1,0:T(8,128)(2,1)S(1)}, bf16[2,128,1152]{2,1,0:T(8,128)(2,1)S(1)}, u32[]{:S(2)}, u32[]{:S(2)}) collective-permute-start(bf16[2,128,1152]{2,1,0:T(8,128)(2,1)S(1)} %shard_map.96), channel_id=1, source_target_pairs={{16,0},{0,16},{48,32},{32,48},{80,64},{64,80},{112,96},{96,112},{1... | collective-permute-start | bytes 1769480 | tf_op jit(solution)/shard_map/ppermute | solution.py:19
  105.6 13.5 %collective-permute-start.25 = (bf16[2,2,16,2304]{3,2,1,0:T(8,128)(2,1)S(1)}, bf16[2,2,16,2304]{3,2,1,0:T(8,128)(2,1)S(1)}, u32[]{:S(2)}, u32[]{:S(2)}) collective-permute-start(bf16[2,2,16,2304]{3,2,1,0:T(8,128)(2,1)S(1)} %get-tuple-element.21), channel_id=1, source_target_pairs={{8,0},{9,1},{10,2},{11,3},{12,4},{13,5},{14,6},{15,7},{0,8},{1,9},... | collective-permute-start | bytes 884744 | tf_op jit(solution)/shard_map/ppermute | solution.py:14
  108.6 13.8 %collective-permute-start.27 = (bf16[2,2,16,2304]{3,2,1,0:T(8,128)(2,1)S(1)}, bf16[2,2,16,2304]{3,2,1,0:T(8,128)(2,1)S(1)}, u32[]{:S(2)}, u32[]{:S(2)}) collective-permute-start(bf16[2,2,16,2304]{3,2,1,0:T(8,128)(2,1)S(1)} %get-tuple-element.22), channel_id=1, source_target_pairs={{12,0},{13,1},{14,2},{15,3},{8,4},{9,5},{10,6},{11,7},{4,8},{5,9},... | collective-permute-start | bytes 884744 | tf_op jit(solution)/shard_map/ppermute | solution.py:14
  109.3 13.1 %collective-permute-start.26 = (bf16[2,2,16,2304]{3,2,1,0:T(8,128)(2,1)S(1)}, bf16[2,2,16,2304]{3,2,1,0:T(8,128)(2,1)S(1)}, u32[]{:S(2)}, u32[]{:S(2)}) collective-permute-start(bf16[2,2,16,2304]{3,2,1,0:T(8,128)(2,1)S(1)} %get-tuple-element.23), channel_id=1, source_target_pairs={{4,0},{5,1},{6,2},{7,3},{0,4},{1,5},{2,6},{3,7},{12,8},{13,9},{14,... | collective-permute-start | bytes 884744 | tf_op jit(solution)/shard_map/ppermute | solution.py:14
  119.1 3.5 %copy-start.5 = (bf16[2,128,1152]{2,1,0:T(8,128)(2,1)}, bf16[2,128,1152]{2,1,0:T(8,128)(2,1)S(1)}, u32[]{:S(2)}) copy-start(bf16[2,128,1152]{2,1,0:T(8,128)(2,1)S(1)} %collective-permute-done.24.refs_2_) | copy-start | bytes 1769476
  122.6 7.7 %collective-permute-start.28 = (bf16[2,2,16,2304]{3,2,0,1:T(8,128)(2,1)S(1)}, bf16[2,2,16,2304]{3,2,0,1:T(8,128)(2,1)S(1)}, u32[]{:S(2)}, u32[]{:S(2)}) collective-permute-start(bf16[2,2,16,2304]{3,2,0,1:T(8,128)(2,1)S(1)} %fusion.23), channel_id=1, source_target_pairs={{2,0},{3,1},{0,2},{1,3},{6,4},{7,5},{4,6},{5,7},{10,8},{11,9},{8,1... | collective-permute-start | bytes 884744 | tf_op jit(solution)/shard_map/ppermute | solution.py:14
  130.6 4.6 %collective-permute-start.32 = (bf16[2,2,16,576]{3,2,0,1:T(8,128)(2,1)S(1)}, bf16[2,2,16,576]{3,2,0,1:T(8,128)(2,1)S(1)}, u32[]{:S(2)}, u32[]{:S(2)}) collective-permute-start(bf16[2,2,16,576]{3,2,0,1:T(8,128)(2,1)S(1)} %get-tuple-element.48), channel_id=1, source_target_pairs={{48,0},{32,16},{16,32},{0,48},{112,64},{96,80},{80,96},{64,112},{4... | collective-permute-start | bytes 221192 | tf_op jit(solution)/shard_map/ppermute | solution.py:19
  131.9 4.8 %collective-permute-start.31 = (bf16[2,2,16,576]{3,2,0,1:T(8,128)(2,1)S(1)}, bf16[2,2,16,576]{3,2,0,1:T(8,128)(2,1)S(1)}, u32[]{:S(2)}, u32[]{:S(2)}) collective-permute-start(bf16[2,2,16,576]{3,2,0,1:T(8,128)(2,1)S(1)} %get-tuple-element.49), channel_id=1, source_target_pairs={{32,0},{48,16},{0,32},{16,48},{96,64},{112,80},{64,96},{80,112},{3... | collective-permute-start | bytes 221192 | tf_op jit(solution)/shard_map/ppermute | solution.py:19
  133.0 3.9 %collective-permute-start.30 = (bf16[2,2,16,576]{3,2,0,1:T(8,128)(2,1)S(1)}, bf16[2,2,16,576]{3,2,0,1:T(8,128)(2,1)S(1)}, u32[]{:S(2)}, u32[]{:S(2)}) collective-permute-start(bf16[2,2,16,576]{3,2,0,1:T(8,128)(2,1)S(1)} %get-tuple-element.50), channel_id=1, source_target_pairs={{16,0},{0,16},{48,32},{32,48},{80,64},{64,80},{112,96},{96,112},{1... | collective-permute-start | bytes 221192 | tf_op jit(solution)/shard_map/ppermute | solution.py:19
  134.0 6.9 %collective-permute-start.29 = (bf16[2,16,2304]{2,1,0:T(8,128)(2,1)S(1)}, bf16[2,16,2304]{2,1,0:T(8,128)(2,1)S(1)}, u32[]{:S(2)}, u32[]{:S(2)}) collective-permute-start(bf16[2,16,2304]{2,1,0:T(8,128)(2,1)S(1)} %fusion.30), channel_id=1, source_target_pairs={{2,0},{3,1},{0,2},{1,3},{6,4},{7,5},{4,6},{5,7},{10,8},{11,9},{8,1... | collective-permute-start | bytes 442376 | tf_op jit(solution)/shard_map/ppermute | solution.py:14
  137.7 8.5 %collective-permute-start.36 = (bf16[2,2,4,16,576]{4,3,2,1,0:T(8,128)(2,1)S(1)}, bf16[2,2,4,16,576]{4,3,2,1,0:T(8,128)(2,1)}, u32[]{:S(2)}, u32[]{:S(2)}) collective-permute-start(bf16[2,2,4,16,576]{4,3,2,1,0:T(8,128)(2,1)S(1)} %get-tuple-element.40.refs_1_), channel_id=1, source_target_pairs={{12,0},{13,1},{14,2},{15,3},{8,4},{9,5},{10,6},{11,7},{4,8},{5,9},... | collective-permute-start | bytes 884744 | tf_op jit(solution)/shard_map/ppermute | solution.py:14
  140.9 6.5 %collective-permute-start.35 = (bf16[2,2,4,16,576]{4,3,2,1,0:T(8,128)(2,1)S(1)}, bf16[2,2,4,16,576]{4,3,2,1,0:T(8,128)(2,1)}, u32[]{:S(2)}, u32[]{:S(2)}) collective-permute-start(bf16[2,2,4,16,576]{4,3,2,1,0:T(8,128)(2,1)S(1)} %get-tuple-element.40.refs_1_), channel_id=1, source_target_pairs={{4,0},{5,1},{6,2},{7,3},{0,4},{1,5},{2,6},{3,7},{12,8},{13,9},{14,... | collective-permute-start | bytes 884744 | tf_op jit(solution)/shard_map/ppermute | solution.py:14
  141.0 11.4 %collective-permute-start.33 = (bf16[2,2,4,16,576]{4,3,2,1,0:T(8,128)(2,1)S(1)}, bf16[2,2,4,16,576]{4,3,2,1,0:T(8,128)(2,1)S(1)}, u32[]{:S(2)}, u32[]{:S(2)}) collective-permute-start(bf16[2,2,4,16,576]{4,3,2,1,0:T(8,128)(2,1)S(1)} %get-tuple-element.40.refs_1_), channel_id=1, source_target_pairs={{1,0},{0,1},{3,2},{2,3},{5,4},{4,5},{7,6},{6,7},{9,8},{8,9},{11,10... | collective-permute-start | bytes 884744 | tf_op jit(solution)/shard_map/ppermute | solution.py:14
  147.2 9.1 %collective-permute-start.37 = (bf16[1,2,4,16,576]{4,3,2,1,0:T(8,128)(2,1)S(1)}, bf16[1,2,4,16,576]{4,3,2,1,0:T(8,128)(2,1)S(1)}, u32[]{:S(2)}, u32[]{:S(2)}) collective-permute-start(bf16[1,2,4,16,576]{4,3,2,1,0:T(8,128)(2,1)S(1)} %slice.271), channel_id=1, source_target_pairs={{4,0},{5,1},{6,2},{7,3},{0,4},{1,5},{2,6},{3,7},{12,8},{13,9},{14,... | collective-permute-start | bytes 442376 | tf_op jit(solution)/shard_map/ppermute | solution.py:14
  148.3 13.3 %collective-permute-start.38 = (bf16[1,2,4,16,576]{4,3,2,1,0:T(8,128)(2,1)S(1)}, bf16[1,2,4,16,576]{4,3,2,1,0:T(8,128)(2,1)S(1)}, u32[]{:S(2)}, u32[]{:S(2)}) collective-permute-start(bf16[1,2,4,16,576]{4,3,2,1,0:T(8,128)(2,1)S(1)} %slice.272), channel_id=1, source_target_pairs={{12,0},{13,1},{14,2},{15,3},{8,4},{9,5},{10,6},{11,7},{4,8},{5,9},... | collective-permute-start | bytes 442376 | tf_op jit(solution)/shard_map/ppermute | solution.py:14
  151.0 15.8 %collective-permute-start.43 = (bf16[2,128,1152]{2,1,0:T(8,128)(2,1)S(1)}, bf16[2,128,1152]{2,1,0:T(8,128)(2,1)}, u32[]{:S(2)}, u32[]{:S(2)}) collective-permute-start(bf16[2,128,1152]{2,1,0:T(8,128)(2,1)S(1)} %shard_map.100), channel_id=1, source_target_pairs={{48,0},{32,16},{16,32},{0,48},{112,64},{96,80},{80,96},{64,112},{4... | collective-permute-start | bytes 1769480 | tf_op jit(solution)/shard_map/ppermute | solution.py:19
  152.2 14.6 %collective-permute-start.42 = (bf16[2,128,1152]{2,1,0:T(8,128)(2,1)S(1)}, bf16[2,128,1152]{2,1,0:T(8,128)(2,1)}, u32[]{:S(2)}, u32[]{:S(2)}) collective-permute-start(bf16[2,128,1152]{2,1,0:T(8,128)(2,1)S(1)} %shard_map.99), channel_id=1, source_target_pairs={{16,0},{0,16},{48,32},{32,48},{80,64},{64,80},{112,96},{96,112},{1... | collective-permute-start | bytes 1769480 | tf_op jit(solution)/shard_map/ppermute | solution.py:19
  152.4 0.7 copy-start.7
  153.1 13.7 %copy-start.2 = (bf16[2,128,1152]{2,1,0:T(8,128)(2,1)S(1)}, bf16[2,128,1152]{2,1,0:T(8,128)(2,1)}, u32[]{:S(2)}) copy-start(bf16[2,128,1152]{2,1,0:T(8,128)(2,1)} %copy-done.1) | copy-start | bytes 1769476
  153.1 13.7 %copy-start.3 = (bf16[1,2,128,1152]{3,2,1,0:T(8,128)(2,1)S(1)}, bf16[1,2,128,1152]{3,2,1,0:T(8,128)(2,1)}, u32[]{:S(2)}) copy-start(bf16[1,2,128,1152]{3,2,1,0:T(8,128)(2,1)} %get-tuple-element.19) | copy-start | bytes 1769476
  153.1 13.7 %copy-start.4 = (bf16[1,2,128,1152]{3,2,1,0:T(8,128)(2,1)S(1)}, bf16[1,2,128,1152]{3,2,1,0:T(8,128)(2,1)}, u32[]{:S(2)}) copy-start(bf16[1,2,128,1152]{3,2,1,0:T(8,128)(2,1)} %get-tuple-element.17) | copy-start | bytes 1769476
  153.1 9.1 %collective-permute-start.34 = (bf16[2,16,2304]{2,1,0:T(8,128)(2,1)S(1)}, bf16[2,16,2304]{2,1,0:T(8,128)(2,1)S(1)}, u32[]{:S(2)}, u32[]{:S(2)}) collective-permute-start(bf16[2,16,2304]{2,1,0:T(8,128)(2,1)S(1)} %shard_map.98), channel_id=1, source_target_pairs={{64,0},{80,16},{96,32},{112,48},{0,64},{16,80},{32,96},{48,112},{6... | collective-permute-start | bytes 442376 | tf_op jit(solution)/shard_map/ppermute | solution.py:19
  156.3 10.5 %collective-permute-start.40 = (bf16[2,2,4,16,576]{4,3,2,1,0:T(8,128)(2,1)}, bf16[2,2,4,16,576]{4,3,2,1,0:T(8,128)(2,1)}, u32[]{:S(2)}, u32[]{:S(2)}) collective-permute-start(bf16[2,2,4,16,576]{4,3,2,1,0:T(8,128)(2,1)} %collective-permute-done.36), channel_id=1, source_target_pairs={{1,0},{0,1},{3,2},{2,3},{5,4},{4,5},{7,6},{6,7},{9,8},{8,9},{11,10... | collective-permute-start | bytes 884744 | tf_op jit(solution)/shard_map/ppermute | solution.py:14
  161.6 5.2 %collective-permute-start.39 = (bf16[2,2,4,16,576]{4,3,2,1,0:T(8,128)(2,1)}, bf16[2,2,4,16,576]{4,3,2,1,0:T(8,128)(2,1)}, u32[]{:S(2)}, u32[]{:S(2)}) collective-permute-start(bf16[2,2,4,16,576]{4,3,2,1,0:T(8,128)(2,1)} %collective-permute-done.35), channel_id=1, source_target_pairs={{1,0},{0,1},{3,2},{2,3},{5,4},{4,5},{7,6},{6,7},{9,8},{8,9},{11,10... | collective-permute-start | bytes 884744 | tf_op jit(solution)/shard_map/ppermute | solution.py:14
  162.3 4.5 %collective-permute-start.41 = (bf16[2,2,4,16,576]{4,3,2,1,0:T(8,128)(2,1)}, bf16[2,2,4,16,576]{4,3,2,1,0:T(8,128)(2,1)}, u32[]{:S(2)}, u32[]{:S(2)}) collective-permute-start(bf16[2,2,4,16,576]{4,3,2,1,0:T(8,128)(2,1)} %constant_dynamic-update-slice_fusion.12), channel_id=1, source_target_pairs={{1,0},{0,1},{3,2},{2,3},{5,4},{4,5},{7,6},{6,7},{9,8},{8,9},{11,10... | collective-permute-start | bytes 884744 | tf_op jit(solution)/shard_map/ppermute | solution.py:14
  166.8 1.1 copy-start.6
  167.9 1.0 copy-start.8
  168.9 1.0 copy-start.9
